TPU v7x, 32 devices: a whole 2x2x4 slice. The times are simulated.
32 devices in a mesh: gx: 4 (over y, core), gy: 8 (over z, x).
Axes of the slice: x: 2, y: 2, z: 4, core: 2. Of those that a mesh axis runs over, the one named last changes fastest.
Arguments:
- tokens: bfloat16 [2, 256, 8192], P(None, None, 'gy'), may hold values from -64 to 64
- cache_lengths: int32 [256], P('gy'), may hold values from 128 to 1024, as said below
- key_cache: bfloat16 [256, 1024, 8, 128], P('gy', None, 'gx'), may hold values from -128 to 128
- value_cache: bfloat16 [256, 1024, 8, 128], P('gy', None, 'gx'), may hold values from -6 to 6
- attn_gain: bfloat16 [8192], P('gy'), may hold values from 0.5 to 1.5
- query_weight: bfloat16 [8192, 8192], P('gy', 'gx'), may hold values from -0.0625 to 0.0625
- keyval_weight: bfloat16 [8192, 2048], P('gy', 'gx'), may hold values from -0.0625 to 0.0625
- out_weight: bfloat16 [8192, 8192], P('gx', 'gy'), may hold values from -0.25 to 0.25
- ffn_gain: bfloat16 [8192], P('gy'), may hold values from 0.5 to 1.5
- gate_weight: bfloat16 [8192, 14336], P('gy', 'gx'), may hold values from -0.0625 to 0.0625
- up_weight: bfloat16 [8192, 14336], P('gy', 'gx'), may hold values from -0.0625 to 0.0625
- down_weight: bfloat16 [14336, 8192], P('gx', 'gy'), may hold values from -0.046875 to 0.046875
Outputs:
- layer_out: bfloat16 [2, 256, 8192], P(None, None, 'gy')
Inputs may be any that keep to these rules, and one draw needn't show every extreme that they name: `cache_lengths`: some sequence has exactly 1024 cached tokens.
All inputs are finite; a program needn't handle non-finite values.
Results may differ from a plain program's by a relative error of at most 0.0095.
Values may be sent and summed in bfloat16 or wider, within the bound.
A program may use at most 192 MiB of HBM per device.

v0:
```python
import math

import jax
import jax.numpy as jnp
from jax import lax
from jax.sharding import PartitionSpec as P

D = 8192
HD = 128
GROUP = 8


epsilon = 1e-05
rotary_base = 500000.0


def rotary(values, positions):
    half_dim = HD // 2
    inv_freq = rotary_base ** (-(jnp.arange(half_dim, dtype=jnp.float32) * 2.0 / HD))
    angles = positions[:, None] * inv_freq[None, :]
    cosine = jnp.cos(angles)[:, None, :]
    sine_part = jnp.sin(angles)[:, None, :]
    first_half = values[..., :half_dim]
    second_half = values[..., half_dim:]
    return jnp.concatenate(
        [
            first_half * cosine - second_half * sine_part,
            second_half * cosine + first_half * sine_part,
        ],
        axis=-1,
    )


def attend_block(queries, cached_keys, cached_values, lengths, extra_keys, extra_values):
    scale_factor = 1.0 / math.sqrt(HD)
    cached = (
        jnp.einsum("sgjd,stgd->sgjt", queries, cached_keys, preferred_element_type=jnp.float32)
        * scale_factor
    )
    valid = jnp.arange(cached_keys.shape[1])[None, :] < lengths[:, None]
    cached = jnp.where(valid[:, None, None, :], cached, -1e30)
    recent = (
        jnp.einsum("sgjd,segd->sgje", queries, extra_keys, preferred_element_type=jnp.float32)
        * scale_factor
    )
    highest = jnp.maximum(
        jnp.max(cached, axis=-1, keepdims=True), jnp.max(recent, axis=-1, keepdims=True)
    )
    cached_exp = jnp.exp(cached - highest)
    recent_exp = jnp.exp(recent - highest)
    totals = jnp.sum(cached_exp, axis=-1, keepdims=True) + jnp.sum(
        recent_exp, axis=-1, keepdims=True
    )
    cached_probs = (cached_exp / totals).astype(jnp.bfloat16)
    recent_probs = (recent_exp / totals).astype(jnp.bfloat16)
    mixed = jnp.einsum(
        "sgjt,stgd->sgjd", cached_probs, cached_values, preferred_element_type=jnp.float32
    )
    mixed = mixed + jnp.einsum(
        "sgje,segd->sgjd", recent_probs, extra_values, preferred_element_type=jnp.float32
    )
    return mixed.reshape(mixed.shape[0], -1).astype(jnp.bfloat16)


def per_device(
    tokens,
    cache_lengths,
    key_cache,
    value_cache,
    attn_gain,
    query_weight,
    keyval_weight,
    out_weight,
    ffn_gain,
    gate_weight,
    up_weight,
    down_weight,
):
    seq_rows = cache_lengths.shape[0]
    query_cols = query_weight.shape[1]
    heads_local = query_cols // HD
    kv_local = keyval_weight.shape[1] // (2 * HD)
    results = []
    keys_new = []
    values_new = []
    for decode_step in range(2):
        current = tokens[decode_step].astype(jnp.float32)
        attn_sq = lax.psum(jnp.sum(current * current, axis=1), "gy")
        row_scale = lax.rsqrt(attn_sq / D + epsilon)[:, None]
        normed = (current * row_scale * attn_gain.astype(jnp.float32)).astype(jnp.bfloat16)

        def project_rows(first_row, row_count, source=normed):
            return jnp.concatenate(
                [
                    jnp.dot(source, query_weight, preferred_element_type=jnp.float32),
                    jnp.dot(source, keyval_weight, preferred_element_type=jnp.float32),
                ],
                axis=1,
            )

        projected = lax.psum_scatter(
            project_rows(jnp.int32(0), seq_rows * lax.axis_size("gy")),
            "gy",
            scatter_dimension=0,
            tiled=True,
        )
        positions = (cache_lengths + decode_step).astype(jnp.float32)
        queries = rotary(
            projected[:, :query_cols].reshape(seq_rows, heads_local, HD), positions
        ).astype(jnp.bfloat16)
        key_value = projected[:, query_cols:].reshape(seq_rows, kv_local, 2, HD)
        keys_new.append(rotary(key_value[:, :, 0], positions).astype(jnp.bfloat16))
        values_new.append(key_value[:, :, 1].astype(jnp.bfloat16))
        extra_keys = jnp.stack(keys_new, axis=1)
        extra_values = jnp.stack(values_new, axis=1)
        attended = attend_block(
            queries.reshape(seq_rows, kv_local, GROUP, HD),
            key_cache,
            value_cache,
            cache_lengths,
            extra_keys,
            extra_values,
        )
        partial_out = jnp.dot(
            lax.all_gather(attended, "gy", axis=0, tiled=True),
            out_weight,
            preferred_element_type=jnp.float32,
        )
        attn_sum = lax.psum(partial_out, "gx")
        resid = (current + attn_sum).astype(jnp.bfloat16)
        resid_f = resid.astype(jnp.float32)
        ffn_sq = lax.psum(jnp.sum(resid_f * resid_f, axis=1), "gy")
        ffn_in = (
            resid_f * lax.rsqrt(ffn_sq / D + epsilon)[:, None] * ffn_gain.astype(jnp.float32)
        ).astype(jnp.bfloat16)
        gate_part = jnp.dot(ffn_in, gate_weight, preferred_element_type=jnp.float32)
        up_part = jnp.dot(ffn_in, up_weight, preferred_element_type=jnp.float32)
        gate_sum, up_sum = lax.psum((gate_part, up_part), "gy")
        activated = (jax.nn.silu(gate_sum) * up_sum).astype(jnp.bfloat16)
        down_part = jnp.dot(activated, down_weight, preferred_element_type=jnp.float32)
        down_sum = lax.psum(down_part.astype(jnp.bfloat16), "gx").astype(jnp.float32)
        results.append((resid_f + down_sum).astype(jnp.bfloat16))
    return jnp.stack(results)


def solution(mesh):
    in_specs = (
        P(None, None, "gy"),
        P("gy"),
        P("gy", None, "gx", None),
        P("gy", None, "gx", None),
        P("gy"),
        P("gy", "gx"),
        P("gy", "gx"),
        P("gx", "gy"),
        P("gy"),
        P("gy", "gx"),
        P("gy", "gx"),
        P("gx", "gy"),
    )
    out_specs = P(None, None, "gy")
    return jax.shard_map(
        per_device, mesh=mesh, in_specs=in_specs, out_specs=out_specs, check_vma=False
    )
```

profile of v0, /device:TPU:0, one launch (start us, length us, event | category | flops | bytes accessed | tf_op | source)
XLA Modules:
  0.0 912.2 jit_solution(13514611149483443171)
XLA Ops:
  6.5 1.6 fusion.31
  8.8 23.1 %all-reduce.1 = (f32[256]{0:T(256)S(1)}, f32[256]{0:T(256)S(1)}) all-reduce(f32[256]{0:T(256)S(1)} %get-tuple-element.6, f32[256]{0:T(256)S(1)} %get-tuple-element.5), channel_id=1, replica_groups=mesh['gx'=4,'gy'=8] {'gy'}, use_global_device_ids=true, to_apply=%region_12.13 | all-reduce | flops 512 | bytes 4096 | tf_op jit(solution)/shard_map/psum | solution.py:88
  31.9 1.5 fusion.63
  33.4 3.7 fusion.65
  37.1 1.7 pad_maximum_fusion.1
  39.4 3.5 fusion.69
  43.0 1.7 pad_maximum_fusion
  45.3 61.3 %reduce-scatter.5.cloned.1.call-done = f32[32,2560]{1,0:T(8,128)} async-done(((f32[256,2560]{1,0:T(8,128)}), f32[32,2560]{1,0:T(8,128)}) %reduce-scatter.5.cloned.1.call-update) | async-done | bytes 327696 | tf_op jit(solution)/shard_map/reduce_scatter | solution.py:101
  107.6 71.9 %reduce-scatter.3.cloned.1.call-done = f32[32,2560]{1,0:T(8,128)} async-done(((f32[256,2560]{1,0:T(8,128)}), f32[32,2560]{1,0:T(8,128)}) %reduce-scatter.3.cloned.1.call-update) | async-done | bytes 327696 | tf_op jit(solution)/shard_map/reduce_scatter | solution.py:101
  183.8 11.6 %fusion.8 = (f32[32,2,8]{2,1,0:T(2,128)S(1)}, f32[32,2,8,1024]{3,2,1,0:T(8,128)}) fusion(pred[32,1024]{1,0:T(8,128)(4,1)S(1)} %iota_compare_fusion, bf16[32,1024,2,128]{3,2,1,0:T(2,128)(2,1)} %param.14, bf16[32,2,8,64]{3,2,1,0:T(8,128)(2,1)S(1)} %get-tuple-element.28, bf16[32,2,8,64]{3,2,1,0:T(8,128)(2,1)S(1)} %get-tuple-element.27), kind=kOutput, calls=%fused_computation.18 | convolution fusion | flops 136052224 | bytes 19040256 | tf_op jit(solution)/shard_map/sgjd,stgd->sgjt/dot_general | solution.py:37
  195.5 12.7 %fusion.12 = (f32[32,2,8]{2,1,0:T(2,128)S(1)}, f32[32,2,8]{2,1,0:T(2,128)S(1)}, f32[32,2,8,1024]{3,2,1,0:T(8,128)}) fusion(f32[32,2,8,1024]{3,2,1,0:T(8,128)} %get-tuple-element.48, f32[32,2,8]{2,1,0:T(2,128)S(1)} %copy.74, pred[32,1024]{1,0:T(8,128)(4,1)S(1)} %iota_compare_fusion, bf16[32,1024,2,128]{3,2,1,0:T(2,128)(2,1)} %param.14, ...), kind=kOutput, calls=%fused_computation.22 | convolution fusion | flops 138148864 | bytes 21141504 | tf_op jit(solution)/shard_map/sgjd,stgd->sgjt/dot_general | solution.py:37
  208.5 9.3 %fusion.20 = bf16[32,2,8,128]{3,2,1,0:T(8,128)(2,1)S(1)} fusion(bf16[32,1024,2,128]{3,2,1,0:T(2,128)(2,1)} %param.15, f32[32,2,8,1024]{3,2,1,0:T(8,128)} %get-tuple-element.48, f32[32,2,8]{2,1,0:T(2,128)S(1)} %copy.76, f32[32,2,8]{2,1,0:T(2,128)S(1)} %copy.74, pred[32,1024]{1,0:T(8,128)(4,1)S(1)} %iota_compare_fusion, f32[32,2,128]{2,1,0:T(2,128)S(1)} %copy.80, ...), kind=kOutput, calls=%fused_computation.41 | convolution fusion | flops 137035776 | bytes 19077120 | tf_op jit(solution)/shard_map/sgjt,stgd->sgjd/dot_general | solution.py:56
  219.1 2.3 fusion.13
  221.4 9.4 %fusion = f32[32,2,8,128]{3,2,1,0:T(8,128)S(1)} fusion(bf16[32,1024,2,128]{3,2,1,0:T(2,128)(2,1)} %param.15, f32[32,2,8,1024]{3,2,1,0:T(8,128)} %get-tuple-element.49, f32[32,2,8]{2,1,0:T(2,128)S(1)} %add.111, f32[32,2,8]{2,1,0:T(2,128)S(1)} %max.15, pred[32,1024]{1,0:T(8,128)(4,1)S(1)} %iota_compare_fusion), kind=kOutput, calls=%fused_computation | convolution fusion | flops 136839168 | bytes 19173376 | tf_op jit(solution)/shard_map/sgjt,stgd->sgjd/dot_general | solution.py:56
  231.9 25.8 %all-gather.3.cloned.1.call-done = bf16[256,2048]{1,0:T(8,128)(2,1)} async-done(((bf16[32,2048]{1,0:T(8,128)(2,1)}), bf16[256,2048]{1,0:T(8,128)(2,1)}) %all-gather.3.cloned.1.call-update) | async-done | bytes 1048592 | tf_op jit(solution)/shard_map/all_gather | solution.py:125
  257.7 4.7 fusion.108
  262.4 36.2 %all-gather.5.cloned.1.call-done = bf16[256,2048]{1,0:T(8,128)(2,1)} async-done(((bf16[32,2048]{1,0:T(8,128)(2,1)}), bf16[256,2048]{1,0:T(8,128)(2,1)}) %all-gather.5.cloned.1.call-update) | async-done | bytes 1048592 | tf_op jit(solution)/shard_map/all_gather | solution.py:125
  298.6 4.7 fusion.109
  303.4 50.4 %all-reduce.11.cloned.1.call-done = (f32[256,1024]{1,0:T(8,128)}, f32[256,1024]{1,0:T(8,128)}) async-done(((f32[256,1024]{1,0:T(8,128)}, f32[256,1024]{1,0:T(8,128)}), (f32[256,1024]{1,0:T(8,128)}, f32[256,1024]{1,0:T(8,128)})) %all-reduce.11.cloned.1.call-update) | async-done | bytes 2097168 | tf_op jit(solution)/shard_map/psum | solution.py:129
  353.9 1.9 fusion.23
  355.8 21.6 %all-reduce = (f32[256]{0:T(256)S(1)}, f32[256]{0:T(256)S(1)}) all-reduce(f32[256]{0:T(256)S(1)} %get-tuple-element.25, f32[256]{0:T(256)S(1)} %get-tuple-element.21), channel_id=1, replica_groups=mesh['gx'=4,'gy'=8] {'gy'}, use_global_device_ids=true, to_apply=%region_20.21 | all-reduce | flops 512 | bytes 4096 | tf_op jit(solution)/shard_map/psum | solution.py:132
  377.4 7.2 fusion.55
  384.7 7.2 fusion.57
  391.9 4.0 fusion.51
  395.8 4.0 fusion.53
  399.9 451.9 %all-reduce.9.cloned.1.call-done = (f32[256,3584]{1,0:T(8,128)}, f32[256,3584]{1,0:T(8,128)}, f32[256,3584]{1,0:T(8,128)}, f32[256,3584]{1,0:T(8,128)}) async-done(((f32[256,3584]{1,0:T(8,128)}, f32[256,3584]{1,0:T(8,128)}, f32[256,3584]{1,0:T(8,128)}, f32[256,3584]{1,0:T(8,128)}), (f32[256,3584]{1,0:T(8,128)}, f32[256,3584]{1,0:T(8,128)}, f32[256,3584]{1,0:T(8,128)}, ...) | async-done | bytes 14680080 | tf_op jit(solution)/shard_map/psum | solution.py:138
  851.8 8.4 fusion.14
  860.2 6.4 fusion.15
  866.6 35.2 %all-reduce.13.cloned.1.call-done = (bf16[256,1024]{1,0:T(8,128)(2,1)}, bf16[256,1024]{1,0:T(8,128)(2,1)}) async-done(((bf16[256,1024]{1,0:T(8,128)(2,1)}, bf16[256,1024]{1,0:T(8,128)(2,1)}), (bf16[256,1024]{1,0:T(8,128)(2,1)}, bf16[256,1024]{1,0:T(8,128)(2,1)})) %all-reduce.13.cloned.1.call-update) | async-done | bytes 1048592 | tf_op jit(solution)/shard_map/psum | solution.py:141
  901.8 1.2 fusion.49
  903.0 1.2 fusion.50
  904.2 1.1 pad_maximum_fusion.2
  (92 shorter events, 9.9 us)
Async XLA Ops:
  6.5 25.3 %copy-start = (bf16[1024,512]{1,0:T(8,128)(2,1)S(1)}, bf16[1024,512]{1,0:T(8,128)(2,1)}, u32[]{:S(2)}) copy-start(bf16[1024,512]{1,0:T(8,128)(2,1)} %param.18) | copy-start | bytes 3145732
  6.5 100.1 %reduce-scatter.5.cloned.1.call-start = ((), (), s32[]{:S(2)}) async-start(), calls=%async_computation.4 | async-start | bytes 2949120 | tf_op jit(solution)/shard_map/reduce_scatter | solution.py:101
  37.1 1.8 copy-start.2
  38.9 140.6 %reduce-scatter.3.cloned.1.call-start = ((), (), s32[]{:S(2)}) async-start(), calls=%async_computation.2 | async-start | bytes 2949120 | tf_op jit(solution)/shard_map/reduce_scatter | solution.py:101
  42.9 2.0 copy-start.4
  44.7 213.0 %all-gather.3.cloned.1.call-start = ((), (), s32[]{:S(2)}) async-start(), calls=%async_computation.3 | async-start | bytes 1179648 | tf_op jit(solution)/shard_map/all_gather | solution.py:125
  218.5 80.1 %all-gather.5.cloned.1.call-start = ((), (), s32[]{:S(2)}) async-start(), calls=%async_computation.5 | async-start | bytes 1179648 | tf_op jit(solution)/shard_map/all_gather | solution.py:125
  231.8 122.1 %all-reduce.11.cloned.1.call-start = ((), (), s32[]{:S(2)}) async-start(), calls=%async_computation.7 | async-start | bytes 4194304 | tf_op jit(solution)/shard_map/psum | solution.py:129
  262.4 41.0 %copy-start.3 = (bf16[1024]{0:T(1024)(128)(2,1)S(1)}, bf16[1024]{0:T(1024)(128)(2,1)}, u32[]{:S(2)}) copy-start(bf16[1024]{0:T(1024)(128)(2,1)} %param.20) | copy-start | bytes 6148
  303.4 548.4 %all-reduce.9.cloned.1.call-start = ((), (), s32[]{:S(2)}) async-start(), calls=%async_computation.6 | async-start | bytes 29360128 | tf_op jit(solution)/shard_map/psum | solution.py:138
  377.4 14.4 %slice-start = ((s8[7340032]{0:T(1024)(128)(4,1)}), s8[4194304]{0:T(1024)(128)(4,1)S(1)}, s32[]{:S(2)}) async-start(s8[7340032]{0:T(1024)(128)(4,1)} %bitcast.107), calls=%async_computation.9 | async-start | bytes 8388608
  384.7 7.2 slice-start.1
  384.7 11.2 %slice-start.2 = ((s8[7340032]{0:T(1024)(128)(4,1)}), s8[4194304]{0:T(1024)(128)(4,1)S(1)}, s32[]{:S(2)}) async-start(s8[7340032]{0:T(1024)(128)(4,1)} %bitcast.109), calls=%async_computation.11 | async-start | bytes 8388608
  391.8 4.0 slice-start.3
  399.8 501.9 %all-reduce.13.cloned.1.call-start = ((), (), s32[]{:S(2)}) async-start(), calls=%async_computation.8 | async-start | bytes 2097152 | tf_op jit(solution)/shard_map/psum | solution.py:141
  851.8 8.4 copy-start.5
  851.8 8.4 copy-start.6
  860.1 45.2 %copy-start.1 = (bf16[1024,512]{1,0:T(8,128)(2,1)S(1)}, bf16[1024,512]{1,0:T(8,128)(2,1)}, u32[]{:S(2)}) copy-start(bf16[1024,512]{1,0:T(8,128)(2,1)} %param.18) | copy-start | bytes 3145732
Sparse Core Ops, SparseCore 0:
  39.0 67.5 reduce-scatter.4
  110.1 69.3 reduce-scatter.2
  218.6 39.0 all-gather.2
  259.7 38.8 all-gather.4
  303.5 50.3 all-reduce.10
  400.0 451.7 all-reduce.8
  866.7 35.0 all-reduce.12
where the time goes:
time: 913 us; the launch traced here: 912 us
  waiting for transfers between devices  733 us (80%)
  matrix products  99.7 us (11%)
  blocking collectives  44.7 us (5%)
  other arithmetic  14.6 us (2%)
  between operations  13.9 us (2%)
    psum x1, waiting for transfers between devices, per_device(): gate_sum, up_sum = lax.psum((gate_part, up_part), 'gy')  452 us
    reduce_scatter x2, waiting for transfers between devices, per_device(): lax.psum_scatter(project_rows(jnp.int32(0), seq_rows * lax.axis_size('gy'...  133 us
    all_gather x2, waiting for transfers between devices, per_device(): lax.all_gather(attended, 'gy', axis=0, tiled=True)  62 us
    psum x1, waiting for transfers between devices, per_device(): attn_sum = lax.psum(partial_out, 'gx')  50.4 us
    psum x1, waiting for transfers between devices, per_device(): lax.psum(down_part.astype(jnp.bfloat16), 'gx').astype(jnp.float32)  35.2 us
    dot_general x2, matrix products, attend_block(): jnp.einsum('sgjd,stgd->sgjt', queries, cached_keys, preferred_element_typ...  24.3 us
    psum x1, blocking collectives, per_device(): attn_sq = lax.psum(jnp.sum(current * current, axis=1), 'gy')  23.1 us
    psum x1, blocking collectives, per_device(): ffn_sq = lax.psum(jnp.sum(resid_f * resid_f, axis=1), 'gy')  21.6 us
  transfers between devices with their start and end apart: 7, of which 7 were waited for; matrix products, arithmetic and copies ran while one was open for 3% of the time, Pallas kernels for 0%

commit v1 on v0

v1 whole, which is shorter than its diff:
```python
import functools
import math

import jax
import jax.numpy as jnp
from jax import lax
from jax.experimental import pallas as pl
from jax.experimental.pallas import tpu as pltpu
from jax.sharding import PartitionSpec as P

HD = 128
GROUP = 8
EXTRA = 128
VMEM_LIMIT = 56 * 1024 * 1024
MESH = pl.DeviceIdType.MESH

epsilon = 1e-05
rotary_base = 500000.0


def remote(src, dst, send, recv, axis, device):
    return pltpu.make_async_remote_copy(
        src_ref=src,
        dst_ref=dst,
        send_sem=send,
        recv_sem=recv,
        device_id={axis: device},
        device_id_type=MESH,
    )


def enter(axis, peers):
    barrier = pltpu.get_barrier_semaphore()
    for peer in peers:
        pl.semaphore_signal(barrier, inc=1, device_id={axis: peer}, device_id_type=MESH)
    pl.semaphore_wait(barrier, len(peers))


def scatter_kernel(n, parts, p_ref, out_ref, near, going, far, ns, nr, fs, fr):
    outer = n // 2
    me = lax.axis_index("gy")
    o, i = me // 2, lax.rem(me, 2)
    partner = me + 1 - 2 * i
    across = [lax.rem(o + k, outer) for k in range(outer)]
    enter("gy", [partner] + [across[k] * 2 + i for k in range(1, outer)])
    width = p_ref.shape[2] // parts
    order = [(s, (k + 1) % outer) for s in range(parts) for k in range(outer)]
    near_copies, far_copies = [], []

    def start_near(s, k):
        cols = pl.ds(s * width, width)
        copy = remote(
            p_ref.at[across[k] * 2 + 1 - i, :, cols],
            near.at[k, :, cols],
            ns.at[s, k],
            nr.at[s, k],
            "gy",
            partner,
        )
        copy.start()
        near_copies.append(copy)

    window = 3
    for s, k in order[:window]:
        start_near(s, k)
    for j, (s, k) in enumerate(order):
        cols = pl.ds(s * width, width)
        near_copies[j].wait_recv()
        near_copies[j].wait_send()
        if j + window < len(order):
            start_near(*order[j + window])
        total = p_ref[across[k] * 2 + i, :, cols].astype(jnp.float32) + near[k, :, cols].astype(
            jnp.float32
        )
        if k == 0:
            out_ref[:, cols] = total
        else:
            going[k - 1, :, cols] = total.astype(jnp.bfloat16)
            copy = remote(
                going.at[k - 1, :, cols],
                far.at[k - 1, :, cols],
                fs.at[s, k - 1],
                fr.at[s, k - 1],
                "gy",
                across[k] * 2 + i,
            )
            copy.start()
            far_copies.append((s, k, copy))
    for s in range(parts):
        cols = pl.ds(s * width, width)
        total = out_ref[:, cols]
        for cs, k, copy in far_copies:
            if cs == s:
                copy.wait_recv()
                total = total + far[k - 1, :, cols].astype(jnp.float32)
        out_ref[:, cols] = total
    for _, _, copy in far_copies:
        copy.wait_send()


def scatter_sum(partial, n, collective_id):
    _, rows, cols = partial.shape
    outer = n // 2
    parts = 3 if cols % 384 == 0 else 1
    return pl.pallas_call(
        functools.partial(scatter_kernel, n, parts),
        out_shape=jax.ShapeDtypeStruct((rows, cols), jnp.float32),
        in_specs=[pl.BlockSpec(memory_space=pltpu.VMEM)],
        out_specs=pl.BlockSpec(memory_space=pltpu.VMEM),
        scratch_shapes=[
            pltpu.VMEM((outer, rows, cols), jnp.bfloat16),
            pltpu.VMEM((outer - 1, rows, cols), jnp.bfloat16),
            pltpu.VMEM((outer - 1, rows, cols), jnp.bfloat16),
            pltpu.SemaphoreType.DMA((parts, outer)),
            pltpu.SemaphoreType.DMA((parts, outer)),
            pltpu.SemaphoreType.DMA((parts, outer - 1)),
            pltpu.SemaphoreType.DMA((parts, outer - 1)),
        ],
        compiler_params=pltpu.CompilerParams(
            collective_id=collective_id, has_side_effects=True, vmem_limit_bytes=VMEM_LIMIT
        ),
    )(partial)


def gather_kernel(n, a_ref, out_ref, own, ns, nr, fs, fr):
    outer = n // 2
    me = lax.axis_index("gy")
    o, i = me // 2, lax.rem(me, 2)
    partner = me + 1 - 2 * i
    across = [lax.rem(o + k, outer) * 2 + i for k in range(outer)]
    behind = [lax.rem(o + outer - k, outer) * 2 + i for k in range(outer)]
    enter("gy", [partner] + across[1:])
    far_copies, near_copies = [], []
    for k in range(1, outer):
        copy = remote(a_ref, out_ref.at[me], fs.at[k - 1], fr.at[k - 1], "gy", across[k])
        copy.start()
        far_copies.append(copy)
    copy = remote(a_ref, out_ref.at[me], ns.at[0], nr.at[0], "gy", partner)
    copy.start()
    near_copies.append(copy)
    mine = pltpu.make_async_copy(a_ref, out_ref.at[me], own)
    mine.start()
    for k in range(1, outer):
        far_copies[k - 1].wait_recv()
        block = out_ref.at[behind[k]]
        copy = remote(block, block, ns.at[k], nr.at[k], "gy", partner)
        copy.start()
        near_copies.append(copy)
    for copy in near_copies:
        copy.wait_recv()
    for copy in far_copies + near_copies:
        copy.wait_send()
    mine.wait()


def gather_rows(block, n, collective_id):
    rows, cols = block.shape
    outer = n // 2
    return pl.pallas_call(
        functools.partial(gather_kernel, n),
        out_shape=jax.ShapeDtypeStruct((n, rows, cols), block.dtype),
        in_specs=[pl.BlockSpec(memory_space=pltpu.VMEM)],
        out_specs=pl.BlockSpec(memory_space=pltpu.VMEM),
        scratch_shapes=[
            pltpu.SemaphoreType.DMA,
            pltpu.SemaphoreType.DMA((outer,)),
            pltpu.SemaphoreType.DMA((outer,)),
            pltpu.SemaphoreType.DMA((outer - 1,)),
            pltpu.SemaphoreType.DMA((outer - 1,)),
        ],
        compiler_params=pltpu.CompilerParams(
            collective_id=collective_id, has_side_effects=True, vmem_limit_bytes=VMEM_LIMIT
        ),
    )(block)


def residual_kernel(n, p_ref, base_ref, out_ref, got, ss, sr, gs, gr):
    me = lax.axis_index("gx")
    across = [lax.rem(me + k, n) for k in range(n)]
    enter("gx", across[1:])
    sums, shares = [], []
    for k in range(1, n):
        copy = remote(
            p_ref.at[across[k]], got.at[k - 1], ss.at[k - 1], sr.at[k - 1], "gx", across[k]
        )
        copy.start()
        sums.append(copy)
    total = p_ref[me].astype(jnp.float32)
    for k in range(1, n):
        sums[k - 1].wait_recv()
        total = total + got[k - 1].astype(jnp.float32)
    out_ref[me] = (base_ref[me].astype(jnp.float32) + total).astype(jnp.bfloat16)
    for k in range(1, n):
        copy = remote(
            out_ref.at[me], out_ref.at[me], gs.at[k - 1], gr.at[k - 1], "gx", across[k]
        )
        copy.start()
        shares.append(copy)
    for copy in shares:
        copy.wait_recv()
    for copy in sums + shares:
        copy.wait_send()


def add_residual(partial, base, n, collective_id):
    rows, cols = partial.shape
    shape = (n, rows // n, cols)
    result = pl.pallas_call(
        functools.partial(residual_kernel, n),
        out_shape=jax.ShapeDtypeStruct(shape, jnp.bfloat16),
        in_specs=[pl.BlockSpec(memory_space=pltpu.VMEM)] * 2,
        out_specs=pl.BlockSpec(memory_space=pltpu.VMEM),
        scratch_shapes=[pltpu.VMEM((n - 1,) + shape[1:], jnp.bfloat16)]
        + [pltpu.SemaphoreType.DMA((n - 1,))] * 4,
        compiler_params=pltpu.CompilerParams(
            collective_id=collective_id, has_side_effects=True, vmem_limit_bytes=VMEM_LIMIT
        ),
    )(partial.reshape(shape), base.reshape(shape))
    return result.reshape(rows, cols)


def rotary(values, positions):
    half_dim = HD // 2
    inv_freq = rotary_base ** (-(jnp.arange(half_dim, dtype=jnp.float32) * 2.0 / HD))
    angles = positions[..., None] * inv_freq
    cosine = jnp.cos(angles)[..., None, :]
    sine_part = jnp.sin(angles)[..., None, :]
    first_half = values[..., :half_dim]
    second_half = values[..., half_dim:]
    return jnp.concatenate(
        [
            first_half * cosine - second_half * sine_part,
            second_half * cosine + first_half * sine_part,
        ],
        axis=-1,
    )


def attend(queries, cached_keys, cached_values, lengths, extra_keys, extra_values):
    seqs, kv, steps = queries.shape[:3]
    flat = queries.reshape(seqs, kv, steps * GROUP, HD)
    scale_factor = 1.0 / math.sqrt(HD)
    cached = (
        jnp.einsum("sgjd,stgd->sgjt", flat, cached_keys, preferred_element_type=jnp.float32)
        * scale_factor
    )
    valid = jnp.arange(cached_keys.shape[1])[None, :] < lengths[:, None]
    cached = jnp.where(valid[:, None, None, :], cached, -1e30)
    recent = (
        jnp.einsum("sgjd,segd->sgje", flat, extra_keys, preferred_element_type=jnp.float32)
        * scale_factor
    )
    step_of = jnp.arange(steps * GROUP) // GROUP
    seen = jnp.arange(steps)[None, :] <= step_of[:, None]
    recent = jnp.where(seen[None, None], recent, -1e30)
    highest = jnp.maximum(
        jnp.max(cached, axis=-1, keepdims=True), jnp.max(recent, axis=-1, keepdims=True)
    )
    cached_exp = jnp.exp(cached - highest)
    recent_exp = jnp.exp(recent - highest)
    totals = jnp.sum(cached_exp, axis=-1, keepdims=True) + jnp.sum(
        recent_exp, axis=-1, keepdims=True
    )
    cached_probs = (cached_exp / totals).astype(jnp.bfloat16)
    recent_probs = (recent_exp / totals).astype(jnp.bfloat16)
    mixed = jnp.einsum(
        "sgjt,stgd->sgjd", cached_probs, cached_values, preferred_element_type=jnp.float32
    )
    mixed = mixed + jnp.einsum(
        "sgje,segd->sgjd", recent_probs, extra_values, preferred_element_type=jnp.float32
    )
    return mixed.reshape(seqs, kv, steps, GROUP, HD).astype(jnp.bfloat16)


def gained(values, gain):
    wide = values.astype(jnp.float32)
    squares = jnp.sum(wide * wide, axis=1, keepdims=True)
    high = squares.astype(jnp.bfloat16)
    low = (squares - high.astype(jnp.float32)).astype(jnp.bfloat16)
    pad = jnp.zeros((values.shape[0], EXTRA - 2), jnp.bfloat16)
    return (wide * gain.astype(jnp.float32)).astype(jnp.bfloat16), [high, low, pad]


def project(values, weights, columns, n):
    parts = [
        jnp.dot(values, weight, preferred_element_type=jnp.float32).astype(jnp.bfloat16)
        for weight in weights
    ]
    return jnp.concatenate(parts + columns, axis=1).reshape(n, values.shape[0] // n, -1)


def row_scaled(summed, width):
    squares = summed[:, -EXTRA] + summed[:, 1 - EXTRA]
    return summed[:, :-EXTRA] * lax.rsqrt(squares / width + epsilon)[:, None]


def per_device(
    tokens,
    cache_lengths,
    key_cache,
    value_cache,
    attn_gain,
    query_weight,
    keyval_weight,
    out_weight,
    ffn_gain,
    gate_weight,
    up_weight,
    down_weight,
):
    n, m = lax.axis_size("gy"), lax.axis_size("gx")
    steps, seqs, local = tokens.shape
    width = local * n
    seq_rows = cache_lengths.shape[0]
    query_cols = query_weight.shape[1]
    heads_local = query_cols // HD
    kv_local = keyval_weight.shape[1] // (2 * HD)
    hidden = gate_weight.shape[1]

    current = (
        tokens.reshape(steps, n, seq_rows, local).transpose(1, 0, 2, 3).reshape(steps * seqs, local)
    )
    values, columns = gained(current, attn_gain)
    projected = row_scaled(
        scatter_sum(project(values, [query_weight, keyval_weight], columns, n), n, 0), width
    )
    positions = (cache_lengths[None, :] + jnp.arange(steps)[:, None]).astype(jnp.float32)
    queries = rotary(
        projected[:, :query_cols].reshape(steps, seq_rows, heads_local, HD), positions
    ).astype(jnp.bfloat16)
    key_value = projected[:, query_cols:].reshape(steps, seq_rows, kv_local, 2, HD)
    new_keys = rotary(key_value[:, :, :, 0], positions).astype(jnp.bfloat16)
    new_values = key_value[:, :, :, 1].astype(jnp.bfloat16)
    attended = attend(
        queries.reshape(steps, seq_rows, kv_local, GROUP, HD).transpose(1, 2, 0, 3, 4),
        key_cache,
        value_cache,
        cache_lengths,
        new_keys.transpose(1, 0, 2, 3),
        new_values.transpose(1, 0, 2, 3),
    )
    attended = attended.transpose(2, 0, 1, 3, 4).reshape(steps * seq_rows, query_cols)
    gathered = gather_rows(attended, n, 1).reshape(steps * seqs, query_cols)
    partial_out = jnp.dot(gathered, out_weight, preferred_element_type=jnp.float32)
    resid = add_residual(partial_out.astype(jnp.bfloat16), current, m, 2)

    values, columns = gained(resid, ffn_gain)
    sums = row_scaled(
        scatter_sum(project(values, [gate_weight, up_weight], columns, n), n, 3), width
    )
    activated = (jax.nn.silu(sums[:, :hidden]) * sums[:, hidden:]).astype(jnp.bfloat16)
    gathered = gather_rows(activated, n, 4).reshape(steps * seqs, hidden)
    partial_down = jnp.dot(gathered, down_weight, preferred_element_type=jnp.float32)
    result = add_residual(partial_down.astype(jnp.bfloat16), resid, m, 5)
    return (
        result.reshape(n, steps, seq_rows, local).transpose(1, 0, 2, 3).reshape(steps, seqs, local)
    )


def solution(mesh):
    in_specs = (
        P(None, None, "gy"),
        P("gy"),
        P("gy", None, "gx", None),
        P("gy", None, "gx", None),
        P("gy"),
        P("gy", "gx"),
        P("gy", "gx"),
        P("gx", "gy"),
        P("gy"),
        P("gy", "gx"),
        P("gy", "gx"),
        P("gx", "gy"),
    )
    out_specs = P(None, None, "gy")
    return jax.shard_map(
        per_device, mesh=mesh, in_specs=in_specs, out_specs=out_specs, check_vma=False
    )
```

time: 913 us -> 396 us (0.43)
  the two profiles are of different devices: /device:TPU:0 before, /device:TPU:25 now
where the time goes in v1:
time: 396 us; the launch traced here: 395 us
  Pallas kernels  297 us (75%)
  matrix products  55.6 us (14%)
  local copies, waits for them, and re-layouts  21.7 us (5%)
  other arithmetic  20.6 us (5%)
    pallas_call x2, Pallas kernels, scatter_sum(): pl.pallas_call(functools.partial(scatter_kernel, n, parts), out_shape=jax...  132 us
    pallas_call x2, Pallas kernels, gather_rows(): pl.pallas_call(functools.partial(gather_kernel, n), out_shape=jax.ShapeDt...  106 us
    pallas_call x2, Pallas kernels, add_residual(): pl.pallas_call(functools.partial(residual_kernel, n), out_shape=jax.Shape...  59.5 us
    dot_general x4, matrix products, project(): jnp.dot(values, weight, preferred_element_type=jnp.float32)  18 us
    concatenate x3, local copies, waits for them, and re-layouts, project(): jnp.concatenate(parts + columns, axis=1)  15.8 us
    dot_general x1, matrix products, attend(): jnp.einsum('sgjd,stgd->sgjt', flat, cached_keys, preferred_element_type=j...  12.3 us
    dot_general x1, matrix products, attend(): jnp.einsum('sgjt,stgd->sgjd', cached_probs, cached_values, preferred_elem...  9.34 us
    dot_general x1, matrix products, per_device(): jnp.dot(gathered, down_weight, preferred_element_type=jnp.float32)  9.19 us

profile of v1, /device:TPU:25, one launch (start us, length us, event | category | flops | bytes accessed | tf_op | source)
XLA Modules:
  0.0 395.3 jit_solution(7832863798379019882)
XLA Ops:
  0.0 0.7 add_convert_fusion.2
  0.8 0.7 convert_element_type.161
  1.5 0.7 convert_element_type.178
  2.1 1.5 multiply_reduce_fusion.1
  3.7 0.7 iota_compare_fusion
  5.9 2.5 fusion.33
  8.7 1.5 convolution_convert_fusion.5
  10.8 2.4 convolution_convert_fusion.2
  13.2 3.6 concatenate.34.p_ref
  16.8 37.8 %shard_map.118 = f32[64,2688]{1,0:T(8,128)} custom-call(bf16[8,64,2688]{2,1,0:T(8,128)(2,1)} %concatenate.34.p_ref), custom_call_target="tpu_custom_call" | custom-call | tf_op jit(solution)/shard_map/pallas_call | solution.py:105
  54.6 1.0 rsqrt_reduce_fusion.1
  55.6 1.2 slice_multiply_fusion.2
  58.1 12.3 %fusion.4 = (f32[32,2,16]{2,1,0:T(2,128)S(1)}, f32[32,2,16,1024]{3,2,1,0:T(8,128)}) fusion(pred[32,1024]{1,0:T(8,128)(4,1)S(1)} %iota_compare_fusion, bf16[32,1024,2,128]{3,2,1,0:T(2,128)(2,1)} %param.14, bf16[2,32,2,8,64]{4,3,2,1,0:T(8,128)(2,1)S(1)} %get-tuple-element.8, bf16[2,32,2,8,64]{4,3,2,1,0:T(8,128)(2,1)S(1)} %get-tuple-element.7), kind=kOutput, calls=%fused_computation.9 | convolution fusion | flops 272104448 | bytes 21270528 | tf_op jit(solution)/shard_map/sgjd,stgd->sgjt/dot_general | solution.py:244
  70.6 3.5 fusion.5
  74.1 9.3 %fusion = f32[32,2,16,128]{3,2,1,0:T(8,128)S(1)} fusion(bf16[32,1024,2,128]{3,2,1,0:T(2,128)(2,1)} %param.15, f32[32,2,16,1024]{3,2,1,0:T(8,128)S(1)} %copy-done.2, f32[32,2,16]{2,1,0:T(2,128)S(1)} %add.66, f32[32,2,16]{2,1,0:T(2,128)S(1)} %max.8, pred[32,1024]{1,0:T(8,128)(4,1)S(1)} %iota_compare_fusion), kind=kOutput, calls=%fused_computation | convolution fusion | flops 273678336 | bytes 21536768 | tf_op jit(solution)/shard_map/sgjt,stgd->sgjd/dot_general | solution.py:266
  83.8 0.8 reshape.227.a_ref
  84.7 38.0 %shard_map.119 = bf16[8,64,2048]{2,1,0:T(8,128)(2,1)} custom-call(bf16[64,2048]{1,0:T(8,128)(2,1)} %reshape.227.a_ref), custom_call_target="tpu_custom_call" | custom-call | tf_op jit(solution)/shard_map/pallas_call | solution.py:159
  122.7 6.1 %convolution_convert_fusion.4 = bf16[512,1024]{1,0:T(8,128)(2,1)} fusion(bf16[512,2048]{1,0:T(8,128)(2,1)} %bitcast.87, bf16[2048,1024]{1,0:T(8,128)(2,1)} %param.19), kind=kOutput, calls=%fused_computation.25 | convolution fusion | flops 2148007936 | bytes 7340032 | tf_op jit(solution)/shard_map/dot_general | solution.py:344
  128.8 30.8 %shard_map.120.base_ref = bf16[4,128,1024]{2,1,0:T(8,128)(2,1)} custom-call(bf16[4,128,1024]{2,1,0:T(8,128)(2,1)} %bitcast.89, bf16[4,128,1024]{2,1,0:T(8,128)(2,1)} %bitcast.82), custom_call_target="tpu_custom_call" | custom-call | tf_op jit(solution)/shard_map/pallas_call | solution.py:208
  159.6 1.5 multiply_reduce_fusion
  161.8 1.6 fusion.6
  163.4 8.7 %convolution_convert_fusion = bf16[512,3584]{1,0:T(8,128)(2,1)} fusion(bf16[512,1024]{1,0:T(8,128)(2,1)S(1)} %fusion.6, bf16[1024,3584]{1,0:T(8,128)(2,1)} %param.22), kind=kOutput, calls=%fused_computation.4 | convolution fusion | flops 3759931392 | bytes 12058624 | tf_op jit(solution)/shard_map/dot_general | solution.py:286
  172.1 5.4 %convolution_convert_fusion.1 = bf16[512,3584]{1,0:T(8,128)(2,1)} fusion(bf16[512,1024]{1,0:T(8,128)(2,1)S(1)} %fusion.6, bf16[1024,3584]{1,0:T(8,128)(2,1)S(1)} %bitcast.95), kind=kOutput, calls=%fused_computation.5 | convolution fusion | flops 3759931392 | bytes 12058624 | tf_op jit(solution)/shard_map/dot_general | solution.py:286
  177.5 12.1 %concatenate.41.p_ref = bf16[8,64,7296]{2,1,0:T(8,128)(2,1)} concatenate(bf16[8,64,3584]{2,1,0:T(8,128)(2,1)} %bitcast.86, bf16[8,64,3584]{2,1,0:T(8,128)(2,1)} %bitcast.85, bf16[8,64,1]{2,1,0:T(8,128)(2,1)S(1)} %copy.54, bf16[8,64,1]{2,1,0:T(8,128)(2,1)S(1)} %subtract_convert_fusion.1, bf16[8,64,126]{2,1,0:T(8,128)(2,1)S(1)} %concatenate.33), dimensions={2} | concatenate | bytes 14942208 | tf_op jit(solution)/shard_map/concatenate | solution.py:289
  189.6 93.8 %shard_map.121 = f32[64,7296]{1,0:T(8,128)} custom-call(bf16[8,64,7296]{2,1,0:T(8,128)(2,1)} %concatenate.41.p_ref), custom_call_target="tpu_custom_call" | custom-call | tf_op jit(solution)/shard_map/pallas_call | solution.py:105
  283.4 1.0 rsqrt_reduce_fusion
  284.5 1.7 slice_multiply_fusion
  286.2 1.0 fusion.16.a_ref
  287.2 67.9 %shard_map.122 = bf16[8,64,3584]{2,1,0:T(8,128)(2,1)} custom-call(bf16[64,3584]{1,0:T(8,128)(2,1)} %fusion.16.a_ref), custom_call_target="tpu_custom_call" | custom-call | tf_op jit(solution)/shard_map/pallas_call | solution.py:159
  355.1 9.2 %convolution_convert_fusion.3 = bf16[512,1024]{1,0:T(8,128)(2,1)} fusion(bf16[512,3584]{1,0:T(8,128)(2,1)} %bitcast.84, bf16[3584,1024]{1,0:T(8,128)(2,1)} %param.23), kind=kOutput, calls=%fused_computation.24 | convolution fusion | flops 3758620672 | bytes 12058624 | tf_op jit(solution)/shard_map/dot_general | solution.py:353
  364.3 28.7 %shard_map.123 = bf16[4,128,1024]{2,1,0:T(8,128)(2,1)} custom-call(bf16[4,128,1024]{2,1,0:T(8,128)(2,1)} %bitcast.90, bf16[4,128,1024]{2,1,0:T(8,128)(2,1)} %shard_map.120.base_ref), custom_call_target="tpu_custom_call" | custom-call | tf_op jit(solution)/shard_map/pallas_call | solution.py:208
  393.0 2.3 copy.55
  (52 shorter events, 4.7 us)
Async XLA Ops:
  0.0 8.7 %copy-start = (bf16[1024,512]{1,0:T(8,128)(2,1)S(1)}, bf16[1024,512]{1,0:T(8,128)(2,1)}, u32[]{:S(2)}) copy-start(bf16[1024,512]{1,0:T(8,128)(2,1)} %param.18) | copy-start | bytes 3145732
  8.4 2.4 copy-start.5
  10.8 2.4 copy-start.3
  16.8 40.7 %copy-start.4 = (f32[2,32,64]{2,0,1:T(2,128)S(1)}, f32[2,32,64]{2,0,1:T(2,128)}, u32[]{:S(2)}) copy-start(f32[2,32,64]{2,0,1:T(2,128)} %copy.48) | copy-start | bytes 49156
  70.4 3.7 copy-start.2
  161.7 10.3 %slice-start = ((s8[7340032]{0:T(1024)(128)(4,1)}), s8[4194304]{0:T(1024)(128)(4,1)S(1)}, s32[]{:S(2)}) async-start(s8[7340032]{0:T(1024)(128)(4,1)} %bitcast.94), calls=%async_computation | async-start | bytes 8388608
  163.4 8.7 %slice-start.1 = ((s8[7340032]{0:T(1024)(128)(4,1)}), s8[3145728]{0:T(1024)(128)(4,1)S(1)}, s32[]{:S(2)}) async-start(s8[7340032]{0:T(1024)(128)(4,1)} %bitcast.94), calls=%async_computation.1 | async-start | bytes 6291456
  355.1 40.2 %copy-start.1 = (bf16[1024,512]{1,0:T(8,128)(2,1)S(1)}, bf16[1024,512]{1,0:T(8,128)(2,1)}, u32[]{:S(2)}) copy-start(bf16[1024,512]{1,0:T(8,128)(2,1)} %param.18) | copy-start | bytes 3145732

commit v2 on v1

--- a/solution.py
+++ b/solution.py
@@ -36,90 +36,187 @@
     pl.semaphore_wait(barrier, len(peers))
 
 
-def scatter_kernel(n, parts, p_ref, out_ref, near, going, far, ns, nr, fs, fr):
+def project_kernel(n, parts, gather, width, x_ref, sq_ref, w1_ref, w2_ref, *refs):
+    if gather:
+        out_ref, refs = refs[0], refs[1:]
+    else:
+        out1_ref, out2_ref, refs = refs[0], refs[1], refs[2:]
+    w1, w2, p_ref, near, going, far, acc, scale, ws, ns, nr, fs, fr, as_, ar, bs, br = refs
     outer = n // 2
     me = lax.axis_index("gy")
     o, i = me // 2, lax.rem(me, 2)
     partner = me + 1 - 2 * i
     across = [lax.rem(o + k, outer) for k in range(outer)]
+    behind = [lax.rem(o + outer - k, outer) * 2 + i for k in range(outer)]
+    rows = sq_ref.shape[1]
+    a, b = w1.shape[1] // parts, w2.shape[1] // parts
+    size = a + b
+    loads = []
+    for s in range(parts):
+        pair = []
+        for j, (src, dst, c) in enumerate(((w1_ref, w1, a), (w2_ref, w2, b))):
+            cols = pl.ds(s * c, c)
+            copy = pltpu.make_async_copy(src.at[:, cols], dst.at[:, cols], ws.at[s, j])
+            copy.start()
+            pair.append(copy)
+        loads.append(pair)
     enter("gy", [partner] + [across[k] * 2 + i for k in range(1, outer)])
-    width = p_ref.shape[2] // parts
-    order = [(s, (k + 1) % outer) for s in range(parts) for k in range(outer)]
-    near_copies, far_copies = [], []
-
-    def start_near(s, k):
-        cols = pl.ds(s * width, width)
-        copy = remote(
-            p_ref.at[across[k] * 2 + 1 - i, :, cols],
-            near.at[k, :, cols],
-            ns.at[s, k],
-            nr.at[s, k],
-            "gy",
-            partner,
-        )
-        copy.start()
-        near_copies.append(copy)
-
-    window = 3
-    for s, k in order[:window]:
-        start_near(s, k)
-    for j, (s, k) in enumerate(order):
-        cols = pl.ds(s * width, width)
-        near_copies[j].wait_recv()
-        near_copies[j].wait_send()
-        if j + window < len(order):
-            start_near(*order[j + window])
-        total = p_ref[across[k] * 2 + i, :, cols].astype(jnp.float32) + near[k, :, cols].astype(
-            jnp.float32
-        )
-        if k == 0:
-            out_ref[:, cols] = total
-        else:
-            going[k - 1, :, cols] = total.astype(jnp.bfloat16)
+    order = [(k + 1) % outer for k in range(outer)]
+    segments = [(sq_ref, 0, parts * size, EXTRA)]
+    segments += [(p_ref, s * size, s * size, size) for s in range(parts)]
+    near_copies, far_copies, sent = {}, {}, []
+
+    def near_start(g):
+        src, start, place, count = segments[g]
+        for k in order:
             copy = remote(
-                going.at[k - 1, :, cols],
-                far.at[k - 1, :, cols],
-                fs.at[s, k - 1],
-                fr.at[s, k - 1],
+                src.at[across[k] * 2 + 1 - i, :, pl.ds(start, count)],
+                near.at[k, :, pl.ds(place, count)],
+                ns.at[g, k],
+                nr.at[g, k],
                 "gy",
-                across[k] * 2 + i,
+                partner,
             )
             copy.start()
-            far_copies.append((s, k, copy))
-    for s in range(parts):
-        cols = pl.ds(s * width, width)
-        total = out_ref[:, cols]
-        for cs, k, copy in far_copies:
-            if cs == s:
-                copy.wait_recv()
-                total = total + far[k - 1, :, cols].astype(jnp.float32)
-        out_ref[:, cols] = total
-    for _, _, copy in far_copies:
+            near_copies[g, k] = copy
+
+    def near_finish(g):
+        src, start, place, count = segments[g]
+        cols = pl.ds(place, count)
+        for k in order:
+            near_copies[g, k].wait_recv()
+            sent.append(near_copies[g, k])
+            total = src[across[k] * 2 + i, :, pl.ds(start, count)].astype(jnp.float32) + near[
+                k, :, cols
+            ].astype(jnp.float32)
+            if k == 0:
+                acc[:, cols] = total
+            else:
+                going[k - 1, :, cols] = total.astype(jnp.bfloat16)
+                copy = remote(
+                    going.at[k - 1, :, cols],
+                    far.at[k - 1, :, cols],
+                    fs.at[g, k - 1],
+                    fr.at[g, k - 1],
+                    "gy",
+                    across[k] * 2 + i,
+                )
+                copy.start()
+                far_copies[g, k] = copy
+
+    def far_finish(g):
+        place, count = segments[g][2:]
+        cols = pl.ds(place, count)
+        total = acc[:, cols]
+        for k in range(1, outer):
+            far_copies[g, k].wait_recv()
+            sent.append(far_copies[g, k])
+            total = total + far[k - 1, :, cols].astype(jnp.float32)
+        return total
+
+    share_far, share_near = {}, {}
+    near_start(0)
+    for t in range(parts + 3):
+        if t < parts:
+            for copy in loads[t]:
+                copy.wait()
+            x = x_ref[...]
+            for buf, c, skip in ((w1, a, 0), (w2, b, a)):
+                dot = jnp.dot(
+                    x, buf[:, pl.ds(t * c, c)], preferred_element_type=jnp.float32
+                ).astype(jnp.bfloat16)
+                p_ref[:, :, pl.ds(t * size + skip, c)] = dot.reshape(n, rows, c)
+            near_start(t + 1)
+        if t == 0:
+            near_finish(0)
+        if 1 <= t <= parts:
+            near_finish(t)
+        if t == 1:
+            squares = far_finish(0)
+            scale[...] = jnp.broadcast_to(
+                lax.rsqrt((squares[:, 0:1] + squares[:, 1:2]) / width + epsilon), scale.shape
+            )
+        if 2 <= t <= parts + 1:
+            s = t - 2
+            total = far_finish(s + 1) * scale[:, 0:1]
+            if gather:
+                cols = pl.ds(s * a, a)
+                gate, up = total[:, :a], total[:, a:]
+                out_ref[me, :, cols] = (gate / (1.0 + jnp.exp(-gate)) * up).astype(jnp.bfloat16)
+                block = out_ref.at[me, :, cols]
+                for k in range(1, outer):
+                    copy = remote(
+                        block, block, as_.at[s, k - 1], ar.at[s, k - 1], "gy", across[k] * 2 + i
+                    )
+                    copy.start()
+                    share_far[s, k] = copy
+                copy = remote(block, block, bs.at[s, 0], br.at[s, 0], "gy", partner)
+                copy.start()
+                share_near[s, 0] = copy
+            else:
+                out1_ref[:, pl.ds(s * a, a)] = total[:, :a]
+                out2_ref[:, pl.ds(s * b, b)] = total[:, a:]
+        if gather and t >= 3:
+            s = t - 3
+            cols = pl.ds(s * a, a)
+            for k in range(1, outer):
+                share_far[s, k].wait_recv()
+                block = out_ref.at[behind[k], :, cols]
+                copy = remote(block, block, bs.at[s, k], br.at[s, k], "gy", partner)
+                copy.start()
+                share_near[s, k] = copy
+    for copy in share_near.values():
+        copy.wait_recv()
+    for copy in sent + list(share_far.values()) + list(share_near.values()):
         copy.wait_send()
 
 
-def scatter_sum(partial, n, collective_id):
-    _, rows, cols = partial.shape
-    outer = n // 2
-    parts = 3 if cols % 384 == 0 else 1
+def project(values, columns, weights, n, gather, collective_id):
+    total_rows, depth = values.shape
+    rows, outer = total_rows // n, n // 2
+    c1, c2 = weights[0].shape[1], weights[1].shape[1]
+    parts = max(p for p in range(1, 8) if c1 % (128 * p) == 0 and c2 % (128 * p) == 0)
+    if gather:
+        out_shape = jax.ShapeDtypeStruct((n, rows, c1), jnp.bfloat16)
+        out_specs = pl.BlockSpec(memory_space=pltpu.VMEM)
+    else:
+        out_shape = [jax.ShapeDtypeStruct((rows, c), jnp.float32) for c in (c1, c2)]
+        out_specs = [pl.BlockSpec(memory_space=pltpu.VMEM)] * 2
+    cols = c1 + c2
+    wide = cols + EXTRA
+    dma = pltpu.SemaphoreType.DMA
     return pl.pallas_call(
-        functools.partial(scatter_kernel, n, parts),
-        out_shape=jax.ShapeDtypeStruct((rows, cols), jnp.float32),
-        in_specs=[pl.BlockSpec(memory_space=pltpu.VMEM)],
-        out_specs=pl.BlockSpec(memory_space=pltpu.VMEM),
+        functools.partial(project_kernel, n, parts, gather, depth * n),
+        out_shape=out_shape,
+        in_specs=[pl.BlockSpec(memory_space=pltpu.VMEM)] * 2
+        + [pl.BlockSpec(memory_space=pl.ANY)] * 2,
+        out_specs=out_specs,
         scratch_shapes=[
-            pltpu.VMEM((outer, rows, cols), jnp.bfloat16),
-            pltpu.VMEM((outer - 1, rows, cols), jnp.bfloat16),
-            pltpu.VMEM((outer - 1, rows, cols), jnp.bfloat16),
-            pltpu.SemaphoreType.DMA((parts, outer)),
-            pltpu.SemaphoreType.DMA((parts, outer)),
-            pltpu.SemaphoreType.DMA((parts, outer - 1)),
-            pltpu.SemaphoreType.DMA((parts, outer - 1)),
+            pltpu.VMEM((depth, c1), jnp.bfloat16),
+            pltpu.VMEM((depth, c2), jnp.bfloat16),
+            pltpu.VMEM((n, rows, cols), jnp.bfloat16),
+            pltpu.VMEM((outer, rows, wide), jnp.bfloat16),
+            pltpu.VMEM((outer - 1, rows, wide), jnp.bfloat16),
+            pltpu.VMEM((outer - 1, rows, wide), jnp.bfloat16),
+            pltpu.VMEM((rows, wide), jnp.float32),
+            pltpu.VMEM((rows, 128), jnp.float32),
+            dma((parts, 2)),
+            dma((parts + 1, outer)),
+            dma((parts + 1, outer)),
+            dma((parts + 1, outer - 1)),
+            dma((parts + 1, outer - 1)),
+            dma((parts, outer - 1)),
+            dma((parts, outer - 1)),
+            dma((parts, outer)),
+            dma((parts, outer)),
         ],
         compiler_params=pltpu.CompilerParams(
             collective_id=collective_id, has_side_effects=True, vmem_limit_bytes=VMEM_LIMIT
         ),
-    )(partial)
+        cost_estimate=pl.CostEstimate(
+            flops=2 * total_rows * depth * cols, bytes_accessed=2 * depth * cols, transcendentals=0
+        ),
+    )(values, columns.reshape(n, rows, EXTRA), *weights)
 
 
 def gather_kernel(n, a_ref, out_ref, own, ns, nr, fs, fr):
@@ -174,44 +271,76 @@
     )(block)
 
 
-def residual_kernel(n, p_ref, base_ref, out_ref, got, ss, sr, gs, gr):
+def residual_kernel(n, p_ref, base_ref, out_ref, near, going, far, *sems):
+    ns, nr, fs, fr, as_, ar, bs, br = sems
+    outer = n // 2
     me = lax.axis_index("gx")
-    across = [lax.rem(me + k, n) for k in range(n)]
-    enter("gx", across[1:])
-    sums, shares = [], []
-    for k in range(1, n):
-        copy = remote(
-            p_ref.at[across[k]], got.at[k - 1], ss.at[k - 1], sr.at[k - 1], "gx", across[k]
+    o, i = me // 2, lax.rem(me, 2)
+    partner = me + 1 - 2 * i
+    across = [lax.rem(o + k, outer) for k in range(outer)]
+    behind = [lax.rem(o + outer - k, outer) * 2 + i for k in range(outer)]
+    enter("gx", [partner] + [across[k] * 2 + i for k in range(1, outer)])
+    order = [(k + 1) % outer for k in range(outer)]
+    copies, near_copies, far_copies, share_far, share_near = [], {}, {}, {}, {}
+
+    def send(src, dst, send_sem, recv_sem, device):
+        copy = remote(src, dst, send_sem, recv_sem, "gx", device)
+        copy.start()
+        copies.append(copy)
+        return copy
+
+    for k in order:
+        near_copies[k] = send(
+            p_ref.at[across[k] * 2 + 1 - i], near.at[k], ns.at[k], nr.at[k], partner
         )
-        copy.start()
-        sums.append(copy)
-    total = p_ref[me].astype(jnp.float32)
-    for k in range(1, n):
-        sums[k - 1].wait_recv()
-        total = total + got[k - 1].astype(jnp.float32)
+    for k in order:
+        near_copies[k].wait_recv()
+        total = p_ref[across[k] * 2 + i].astype(jnp.float32) + near[k].astype(jnp.float32)
+        if k:
+            going[k - 1] = total.astype(jnp.bfloat16)
+            far_copies[k] = send(
+                going.at[k - 1],
+                far.at[k - 1],
+                fs.at[k - 1],
+                fr.at[k - 1],
+                across[k] * 2 + i,
+            )
+    for k in range(1, outer):
+        far_copies[k].wait_recv()
+        total = total + far[k - 1].astype(jnp.float32)
     out_ref[me] = (base_ref[me].astype(jnp.float32) + total).astype(jnp.bfloat16)
-    for k in range(1, n):
-        copy = remote(
-            out_ref.at[me], out_ref.at[me], gs.at[k - 1], gr.at[k - 1], "gx", across[k]
-        )
-        copy.start()
-        shares.append(copy)
-    for copy in shares:
+    block = out_ref.at[me]
+    for k in range(1, outer):
+        share_far[k] = send(block, block, as_.at[k - 1], ar.at[k - 1], across[k] * 2 + i)
+    share_near[0] = send(block, block, bs.at[0], br.at[0], partner)
+    for k in range(1, outer):
+        share_far[k].wait_recv()
+        block = out_ref.at[behind[k]]
+        share_near[k] = send(block, block, bs.at[k], br.at[k], partner)
+    for copy in share_near.values():
         copy.wait_recv()
-    for copy in sums + shares:
+    for copy in copies:
         copy.wait_send()
 
 
 def add_residual(partial, base, n, collective_id):
     rows, cols = partial.shape
     shape = (n, rows // n, cols)
+    outer = n // 2
+    dma = pltpu.SemaphoreType.DMA
     result = pl.pallas_call(
         functools.partial(residual_kernel, n),
         out_shape=jax.ShapeDtypeStruct(shape, jnp.bfloat16),
         in_specs=[pl.BlockSpec(memory_space=pltpu.VMEM)] * 2,
         out_specs=pl.BlockSpec(memory_space=pltpu.VMEM),
-        scratch_shapes=[pltpu.VMEM((n - 1,) + shape[1:], jnp.bfloat16)]
-        + [pltpu.SemaphoreType.DMA((n - 1,))] * 4,
+        scratch_shapes=[
+            pltpu.VMEM((outer,) + shape[1:], jnp.bfloat16),
+            pltpu.VMEM((outer - 1,) + shape[1:], jnp.bfloat16),
+            pltpu.VMEM((outer - 1,) + shape[1:], jnp.bfloat16),
+        ]
+        + [dma((outer,))] * 2
+        + [dma((outer - 1,))] * 4
+        + [dma((outer,))] * 2,
         compiler_params=pltpu.CompilerParams(
             collective_id=collective_id, has_side_effects=True, vmem_limit_bytes=VMEM_LIMIT
         ),
@@ -278,20 +407,9 @@
     high = squares.astype(jnp.bfloat16)
     low = (squares - high.astype(jnp.float32)).astype(jnp.bfloat16)
     pad = jnp.zeros((values.shape[0], EXTRA - 2), jnp.bfloat16)
-    return (wide * gain.astype(jnp.float32)).astype(jnp.bfloat16), [high, low, pad]
-
-
-def project(values, weights, columns, n):
-    parts = [
-        jnp.dot(values, weight, preferred_element_type=jnp.float32).astype(jnp.bfloat16)
-        for weight in weights
-    ]
-    return jnp.concatenate(parts + columns, axis=1).reshape(n, values.shape[0] // n, -1)
-
-
-def row_scaled(summed, width):
-    squares = summed[:, -EXTRA] + summed[:, 1 - EXTRA]
-    return summed[:, :-EXTRA] * lax.rsqrt(squares / width + epsilon)[:, None]
+    return (wide * gain.astype(jnp.float32)).astype(jnp.bfloat16), jnp.concatenate(
+        [high, low, pad], axis=1
+    )
 
 
 def per_device(
@@ -310,7 +428,6 @@
 ):
     n, m = lax.axis_size("gy"), lax.axis_size("gx")
     steps, seqs, local = tokens.shape
-    width = local * n
     seq_rows = cache_lengths.shape[0]
     query_cols = query_weight.shape[1]
     heads_local = query_cols // HD
@@ -321,14 +438,12 @@
         tokens.reshape(steps, n, seq_rows, local).transpose(1, 0, 2, 3).reshape(steps * seqs, local)
     )
     values, columns = gained(current, attn_gain)
-    projected = row_scaled(
-        scatter_sum(project(values, [query_weight, keyval_weight], columns, n), n, 0), width
-    )
+    query_part, key_value = project(values, columns, [query_weight, keyval_weight], n, False, 0)
     positions = (cache_lengths[None, :] + jnp.arange(steps)[:, None]).astype(jnp.float32)
     queries = rotary(
-        projected[:, :query_cols].reshape(steps, seq_rows, heads_local, HD), positions
+        query_part.reshape(steps, seq_rows, heads_local, HD), positions
     ).astype(jnp.bfloat16)
-    key_value = projected[:, query_cols:].reshape(steps, seq_rows, kv_local, 2, HD)
+    key_value = key_value.reshape(steps, seq_rows, kv_local, 2, HD)
     new_keys = rotary(key_value[:, :, :, 0], positions).astype(jnp.bfloat16)
     new_values = key_value[:, :, :, 1].astype(jnp.bfloat16)
     attended = attend(
@@ -345,11 +460,8 @@
     resid = add_residual(partial_out.astype(jnp.bfloat16), current, m, 2)
 
     values, columns = gained(resid, ffn_gain)
-    sums = row_scaled(
-        scatter_sum(project(values, [gate_weight, up_weight], columns, n), n, 3), width
-    )
-    activated = (jax.nn.silu(sums[:, :hidden]) * sums[:, hidden:]).astype(jnp.bfloat16)
-    gathered = gather_rows(activated, n, 4).reshape(steps * seqs, hidden)
+    activated = project(values, columns, [gate_weight, up_weight], n, True, 3)
+    gathered = activated.reshape(steps * seqs, hidden)
     partial_down = jnp.dot(gathered, down_weight, preferred_element_type=jnp.float32)
     result = add_residual(partial_down.astype(jnp.bfloat16), resid, m, 5)
     return (

time: 396 us -> 323 us (0.82)
  the two profiles are of different devices: /device:TPU:25 before, /device:TPU:0 now
where the time goes in v2:
time: 323 us
  Pallas kernels  262 us (81%)
  matrix products  35.5 us (11%)
  other arithmetic  18.3 us (6%)
  local copies, waits for them, and re-layouts  6.71 us (2%)
    pallas_call x2, Pallas kernels, project(): pl.pallas_call(functools.partial(project_kernel, n, parts, gather, depth...  186 us
    pallas_call x2, Pallas kernels, add_residual(): pl.pallas_call(functools.partial(residual_kernel, n), out_shape=jax.Shape...  42 us
    pallas_call x1, Pallas kernels, gather_rows(): pl.pallas_call(functools.partial(gather_kernel, n), out_shape=jax.ShapeDt...  33.5 us
    dot_general x1, matrix products, attend(): jnp.einsum('sgjd,stgd->sgjt', flat, cached_keys, preferred_element_type=j...  12.3 us
    dot_general x1, matrix products, attend(): jnp.einsum('sgjt,stgd->sgjd', cached_probs, cached_values, preferred_elem...  9.38 us
    dot_general x1, matrix products, per_device(): jnp.dot(gathered, down_weight, preferred_element_type=jnp.float32)  6.96 us

profile of v2, /device:TPU:0, one launch (start us, length us, event | category | flops | bytes accessed | tf_op | source)
XLA Modules:
  0.0 322.7 jit_solution(17517423924992289606)
XLA Ops:
  0.1 0.7 add_convert_fusion.2
  0.8 0.7 convert_element_type.146
  1.5 0.7 convert_element_type.161
  2.1 1.5 multiply_reduce_fusion.1
  3.7 0.7 iota_compare_fusion
  4.5 0.2 multiply_cosine_fusion
  4.8 0.2 copy.42
  5.3 0.8 maximum_maximum_fusion.sq_ref
  6.0 2.5 fusion.32
  8.5 1.2 fusion.7.x_ref
  9.8 43.0 %shard_map.118 = (f32[64,2048]{1,0:T(8,128)}, f32[64,512]{1,0:T(8,128)}) custom-call(bf16[512,1024]{1,0:T(8,128)(2,1)} %fusion.7.x_ref, bf16[8,64,128]{2,1,0:T(8,128)(2,1)} %maximum_maximum_fusion.sq_ref, bf16[1024,2048]{1,0:T(8,128)(2,1)} %w1_ref.2, bf16[1024,512]{1,0:T(8,128)(2,1)} %w2_ref.2), custom_call_target="tpu_custom_call" | custom-call | flops 2684354560 | bytes 5242880 | tf_op jit(solution)/shard_map/pallas_call | solution.py:188
  52.8 1.1 copy.59
  54.0 0.2 fusion.16
  54.2 1.0 reshape.222
  55.4 0.2 subtract_convert_fusion.3
  55.6 0.4 fusion.33
  56.0 12.3 %fusion.4 = (f32[32,2,16]{2,1,0:T(2,128)S(1)}, f32[32,2,16,1024]{3,2,1,0:T(8,128)}) fusion(pred[32,1024]{1,0:T(8,128)(4,1)S(1)} %iota_compare_fusion, bf16[32,1024,2,128]{3,2,1,0:T(2,128)(2,1)} %param.14, bf16[2,32,2,8,64]{4,3,2,1,0:T(8,128)(2,1)S(1)} %get-tuple-element.12, bf16[2,32,2,8,64]{4,3,2,1,0:T(8,128)(2,1)S(1)} %get-tuple-element.11), kind=kOutput, calls=%fused_computation.7 | convolution fusion | flops 272104448 | bytes 21270528 | tf_op jit(solution)/shard_map/sgjd,stgd->sgjt/dot_general | solution.py:373
  68.5 3.7 %fusion.5 = f32[32,2,16]{2,1,0:T(2,128)S(1)} fusion(f32[32,2,16,1024]{3,2,1,0:T(8,128)} %get-tuple-element.18, f32[32,2,16]{2,1,0:T(2,128)S(1)} %max.8, pred[32,1024]{1,0:T(8,128)(4,1)S(1)} %iota_compare_fusion), kind=kLoop, calls=%fused_computation.8 | loop fusion | flops 4193280 | bytes 4235264 | tf_op jit(solution)/shard_map/reduce_sum | solution.py:390
  72.2 9.4 %fusion = f32[32,2,16,128]{3,2,1,0:T(8,128)S(1)} fusion(bf16[32,1024,2,128]{3,2,1,0:T(2,128)(2,1)} %param.15, f32[32,2,16,1024]{3,2,1,0:T(8,128)S(1)} %copy-done, f32[32,2,16]{2,1,0:T(2,128)S(1)} %add.44, f32[32,2,16]{2,1,0:T(2,128)S(1)} %max.8, pred[32,1024]{1,0:T(8,128)(4,1)S(1)} %iota_compare_fusion), kind=kOutput, calls=%fused_computation | convolution fusion | flops 273678336 | bytes 21536768 | tf_op jit(solution)/shard_map/sgjt,stgd->sgjd/dot_general | solution.py:395
  81.6 0.3 fusion.14
  82.0 0.8 reshape.223.a_ref
  82.8 33.5 %shard_map.119 = bf16[8,64,2048]{2,1,0:T(8,128)(2,1)} custom-call(bf16[64,2048]{1,0:T(8,128)(2,1)} %reshape.223.a_ref), custom_call_target="tpu_custom_call" | custom-call | tf_op jit(solution)/shard_map/pallas_call | solution.py:256
  116.3 6.1 %convolution_convert_fusion.1 = bf16[512,1024]{1,0:T(8,128)(2,1)} fusion(bf16[512,2048]{1,0:T(8,128)(2,1)} %bitcast.71, bf16[2048,1024]{1,0:T(8,128)(2,1)} %param.19), kind=kOutput, calls=%fused_computation.21 | convolution fusion | flops 2148007936 | bytes 7340032 | tf_op jit(solution)/shard_map/dot_general | solution.py:459
  122.5 20.9 %shard_map.120.base_ref = bf16[4,128,1024]{2,1,0:T(8,128)(2,1)} custom-call(bf16[4,128,1024]{2,1,0:T(8,128)(2,1)} %bitcast.72, bf16[4,128,1024]{2,1,0:T(8,128)(2,1)} %bitcast.69), custom_call_target="tpu_custom_call" | custom-call | tf_op jit(solution)/shard_map/pallas_call | solution.py:331
  143.4 1.5 multiply_reduce_fusion
  145.0 0.2 copy.54
  145.5 0.8 maximum_maximum_fusion.1.sq_ref
  146.3 2.6 fusion.6.x_ref
  148.9 143.4 %shard_map.121 = bf16[8,64,3584]{2,1,0:T(8,128)(2,1)} custom-call(bf16[512,1024]{1,0:T(8,128)(2,1)} %fusion.6.x_ref, bf16[8,64,128]{2,1,0:T(8,128)(2,1)} %maximum_maximum_fusion.1.sq_ref, bf16[1024,3584]{1,0:T(8,128)(2,1)} %w1_ref.3, bf16[1024,3584]{1,0:T(8,128)(2,1)} %w2_ref.3), custom_call_target="tpu_custom_call" | custom-call | flops 7516192768 | bytes 14680064 | tf_op jit(solution)/shard_map/pallas_call | solution.py:188
  292.4 7.0 %convolution_convert_fusion = bf16[512,1024]{1,0:T(8,128)(2,1)} fusion(bf16[512,3584]{1,0:T(8,128)(2,1)} %bitcast.79, bf16[3584,1024]{1,0:T(8,128)(2,1)S(1)} %bitcast.78), kind=kOutput, calls=%fused_computation.20 | convolution fusion | flops 3758620672 | bytes 12058624 | tf_op jit(solution)/shard_map/dot_general | solution.py:465
  299.3 21.1 %shard_map.122 = bf16[4,128,1024]{2,1,0:T(8,128)(2,1)} custom-call(bf16[4,128,1024]{2,1,0:T(8,128)(2,1)} %bitcast.73, bf16[4,128,1024]{2,1,0:T(8,128)(2,1)} %shard_map.120.base_ref), custom_call_target="tpu_custom_call" | custom-call | tf_op jit(solution)/shard_map/pallas_call | solution.py:331
  320.4 2.3 copy.55
  (31 shorter events, 1.4 us)
Async XLA Ops:
  68.3 3.9 %copy-start = (f32[32,2,16,1024]{3,2,1,0:T(8,128)S(1)}, f32[32,2,16,1024]{3,2,1,0:T(8,128)}, u32[]{:S(2)}) copy-start(f32[32,2,16,1024]{3,2,1,0:T(8,128)} %get-tuple-element.18) | copy-start | bytes 12582916
  146.3 146.0 %slice-start = ((s8[7340032]{0:T(1024)(128)(4,1)}), s8[4194304]{0:T(1024)(128)(4,1)S(1)}, s32[]{:S(2)}) async-start(s8[7340032]{0:T(1024)(128)(4,1)} %bitcast.77), calls=%async_computation | async-start | bytes 8388608
  148.9 143.5 %slice-start.1 = ((s8[7340032]{0:T(1024)(128)(4,1)}), s8[3145728]{0:T(1024)(128)(4,1)S(1)}, s32[]{:S(2)}) async-start(s8[7340032]{0:T(1024)(128)(4,1)} %bitcast.77), calls=%async_computation.1 | async-start | bytes 6291456

commit v3 on v2

--- a/solution.py
+++ b/solution.py
@@ -36,22 +36,73 @@
     pl.semaphore_wait(barrier, len(peers))
 
 
+def flipped(me, r):
+    value = me
+    for j in range(r.bit_length()):
+        if (r >> j) & 1:
+            value = value + (1 << j) * (1 - 2 * lax.rem(me // (1 << j), 2))
+    return value
+
+
+def bit_order(levels, part, parts):
+    order = list(range(levels))
+    return order[1:] + order[:1] if parts > 3 and part == 0 else order
+
+
+class Share:
+    def __init__(self, me, levels, buf, send_sem, recv_sem):
+        self.me, self.levels, self.buf = me, levels, buf
+        self.send_sem, self.recv_sem = send_sem, recv_sem
+        self.copies, self.bits, self.cols, self.helds = {}, {}, {}, {}
+
+    def send(self, s, step, held, r):
+        bit = self.bits[s][step]
+        slot = (1 << step) - 1 + held
+        block = self.buf.at[flipped(self.me, r), :, self.cols[s]]
+        copy = remote(
+            block,
+            block,
+            self.send_sem.at[s, slot],
+            self.recv_sem.at[s, slot],
+            "gy",
+            flipped(self.me, 1 << bit),
+        )
+        copy.start()
+        self.copies[s, step, held] = copy
+
+    def start(self, s, order, cols):
+        self.bits[s], self.cols[s] = order[::-1], cols
+        self.helds[s] = [0]
+        for step in range(self.levels):
+            self.send(s, step, 0, 0)
+
+    def next(self, s, step):
+        bit = self.bits[s][step]
+        held = self.helds[s]
+        for j, r in enumerate(list(held)):
+            self.copies[s, step, j].wait_recv()
+            held.append(r ^ (1 << bit))
+            for later in range(step + 1, self.levels):
+                self.send(s, later, len(held) - 1, held[-1])
+
+    def end(self):
+        for copy in self.copies.values():
+            copy.wait_send()
+
+
 def project_kernel(n, parts, gather, width, x_ref, sq_ref, w1_ref, w2_ref, *refs):
     if gather:
-        out_ref, refs = refs[0], refs[1:]
+        w3_ref, out_ref, w3, full, dsum, ls, as_, ar = refs[0], refs[1], *refs[-6:]
+        refs = refs[2:-6]
     else:
         out1_ref, out2_ref, refs = refs[0], refs[1], refs[2:]
-    w1, w2, p_ref, near, going, far, acc, scale, ws, ns, nr, fs, fr, as_, ar, bs, br = refs
-    outer = n // 2
+    w1, w2, p_ref, cur, got, scale, ws, ss, rs = refs
+    levels = n.bit_length() - 1
     me = lax.axis_index("gy")
-    o, i = me // 2, lax.rem(me, 2)
-    partner = me + 1 - 2 * i
-    across = [lax.rem(o + k, outer) for k in range(outer)]
-    behind = [lax.rem(o + outer - k, outer) * 2 + i for k in range(outer)]
     rows = sq_ref.shape[1]
     a, b = w1.shape[1] // parts, w2.shape[1] // parts
     size = a + b
-    loads = []
+    loads, late_loads = [], []
     for s in range(parts):
         pair = []
         for j, (src, dst, c) in enumerate(((w1_ref, w1, a), (w2_ref, w2, b))):
@@ -60,63 +111,72 @@
             copy.start()
             pair.append(copy)
         loads.append(pair)
-    enter("gy", [partner] + [across[k] * 2 + i for k in range(1, outer)])
-    order = [(k + 1) % outer for k in range(outer)]
+    enter("gy", [flipped(me, 1 << j) for j in range(levels)])
+    if gather:
+        for s in range(parts):
+            lines = pl.ds(s * a, a)
+            copy = pltpu.make_async_copy(w3_ref.at[lines], w3.at[lines], ls.at[s])
+            copy.start()
+            late_loads.append(copy)
+        share = Share(me, levels, full, as_, ar)
     segments = [(sq_ref, 0, parts * size, EXTRA)]
     segments += [(p_ref, s * size, s * size, size) for s in range(parts)]
-    near_copies, far_copies, sent = {}, {}, []
-
-    def near_start(g):
+    orders = [list(range(levels))] + [bit_order(levels, s, parts) for s in range(parts)]
+    kept, copies = {}, {}
+    for g, order in enumerate(orders):
+        kept[g, 0] = list(range(n))
+        for q, bit in enumerate(order):
+            rest = [r for r in kept[g, q] if not (r >> bit) & 1]
+            if q + 1 < levels:
+                rest.sort(key=lambda r: not (r >> order[q + 1]) & 1)
+            kept[g, q + 1] = rest
+
+    def base(q):
+        return n - (n >> q)
+
+    def held(g, q, r):
         src, start, place, count = segments[g]
-        for k in order:
-            copy = remote(
-                src.at[across[k] * 2 + 1 - i, :, pl.ds(start, count)],
-                near.at[k, :, pl.ds(place, count)],
-                ns.at[g, k],
-                nr.at[g, k],
-                "gy",
-                partner,
-            )
-            copy.start()
-            near_copies[g, k] = copy
-
-    def near_finish(g):
-        src, start, place, count = segments[g]
-        cols = pl.ds(place, count)
-        for k in order:
-            near_copies[g, k].wait_recv()
-            sent.append(near_copies[g, k])
-            total = src[across[k] * 2 + i, :, pl.ds(start, count)].astype(jnp.float32) + near[
-                k, :, cols
+        if q == 0:
+            return src, flipped(me, r), pl.ds(start, count)
+        return cur, kept[g, 1].index(r), pl.ds(place, count)
+
+    def send(g, q, r):
+        bit = orders[g][q]
+        place, count = segments[g][2:]
+        src, lead, cols = held(g, q, r ^ (1 << bit))
+        slot = base(q) + kept[g, q + 1].index(r)
+        copy = remote(
+            src.at[lead, :, cols],
+            got.at[slot, :, pl.ds(place, count)],
+            ss.at[g, slot],
+            rs.at[g, slot],
+            "gy",
+            flipped(me, 1 << bit),
+        )
+        copy.start()
+        copies[g, q, r] = copy
+
+    def first(g):
+        for r in kept[g, 1]:
+            send(g, 0, r)
+
+    def finish(g, q):
+        place, count = segments[g][2:]
+        for j, r in enumerate(kept[g, q + 1]):
+            copies[g, q, r].wait_recv()
+            src, lead, cols = held(g, q, r)
+            total = src[lead, :, cols].astype(jnp.float32) + got[
+                base(q) + j, :, pl.ds(place, count)
             ].astype(jnp.float32)
-            if k == 0:
-                acc[:, cols] = total
-            else:
-                going[k - 1, :, cols] = total.astype(jnp.bfloat16)
-                copy = remote(
-                    going.at[k - 1, :, cols],
-                    far.at[k - 1, :, cols],
-                    fs.at[g, k - 1],
-                    fr.at[g, k - 1],
-                    "gy",
-                    across[k] * 2 + i,
-                )
-                copy.start()
-                far_copies[g, k] = copy
-
-    def far_finish(g):
-        place, count = segments[g][2:]
-        cols = pl.ds(place, count)
-        total = acc[:, cols]
-        for k in range(1, outer):
-            far_copies[g, k].wait_recv()
-            sent.append(far_copies[g, k])
-            total = total + far[k - 1, :, cols].astype(jnp.float32)
+            if q + 1 < levels:
+                cur[kept[g, 1].index(r), :, pl.ds(place, count)] = total.astype(jnp.bfloat16)
+                bit = orders[g][q + 1]
+                if (r >> bit) & 1:
+                    send(g, q + 1, r ^ (1 << bit))
         return total
 
-    share_far, share_near = {}, {}
-    near_start(0)
-    for t in range(parts + 3):
+    first(0)
+    for t in range(parts + 1 + 2 * levels):
         if t < parts:
             for copy in loads[t]:
                 copy.wait()
@@ -126,90 +186,103 @@
                     x, buf[:, pl.ds(t * c, c)], preferred_element_type=jnp.float32
                 ).astype(jnp.bfloat16)
                 p_ref[:, :, pl.ds(t * size + skip, c)] = dot.reshape(n, rows, c)
-            near_start(t + 1)
-        if t == 0:
-            near_finish(0)
-        if 1 <= t <= parts:
-            near_finish(t)
-        if t == 1:
-            squares = far_finish(0)
-            scale[...] = jnp.broadcast_to(
-                lax.rsqrt((squares[:, 0:1] + squares[:, 1:2]) / width + epsilon), scale.shape
-            )
-        if 2 <= t <= parts + 1:
-            s = t - 2
-            total = far_finish(s + 1) * scale[:, 0:1]
+            first(t + 1)
+        if t < levels:
+            squares = finish(0, t)
+            if t == levels - 1:
+                scale[...] = jnp.broadcast_to(
+                    lax.rsqrt((squares[:, 0:1] + squares[:, 1:2]) / width + epsilon), scale.shape
+                )
+        for q in range(levels):
+            s = t - 1 - q
+            if not 0 <= s < parts:
+                continue
+            total = finish(s + 1, q)
+            if q + 1 < levels:
+                continue
+            total = total * scale[:, 0:1]
             if gather:
                 cols = pl.ds(s * a, a)
                 gate, up = total[:, :a], total[:, a:]
-                out_ref[me, :, cols] = (gate / (1.0 + jnp.exp(-gate)) * up).astype(jnp.bfloat16)
-                block = out_ref.at[me, :, cols]
-                for k in range(1, outer):
-                    copy = remote(
-                        block, block, as_.at[s, k - 1], ar.at[s, k - 1], "gy", across[k] * 2 + i
-                    )
-                    copy.start()
-                    share_far[s, k] = copy
-                copy = remote(block, block, bs.at[s, 0], br.at[s, 0], "gy", partner)
-                copy.start()
-                share_near[s, 0] = copy
+                full[me, :, cols] = (gate / (1.0 + jnp.exp(-gate)) * up).astype(jnp.bfloat16)
+                share.start(s, orders[s + 1], cols)
             else:
                 out1_ref[:, pl.ds(s * a, a)] = total[:, :a]
                 out2_ref[:, pl.ds(s * b, b)] = total[:, a:]
-        if gather and t >= 3:
-            s = t - 3
-            cols = pl.ds(s * a, a)
-            for k in range(1, outer):
-                share_far[s, k].wait_recv()
-                block = out_ref.at[behind[k], :, cols]
-                copy = remote(block, block, bs.at[s, k], br.at[s, k], "gy", partner)
-                copy.start()
-                share_near[s, k] = copy
-    for copy in share_near.values():
-        copy.wait_recv()
-    for copy in sent + list(share_far.values()) + list(share_near.values()):
+        if gather:
+            for step in range(levels):
+                s = t - 1 - levels - step
+                if 0 <= s < parts:
+                    share.next(s, step)
+                    if step == levels - 1:
+                        late_loads[s].wait()
+                        add_part(full, w3, dsum, out_ref, s, parts)
+    for copy in copies.values():
         copy.wait_send()
-
-
-def project(values, columns, weights, n, gather, collective_id):
+    if gather:
+        share.end()
+
+
+def add_part(full, weight, dsum, out_ref, s, parts):
+    n, rows, cols = full.shape
+    c = cols // parts
+    dot = jnp.dot(
+        full[:, :, pl.ds(s * c, c)].reshape(n * rows, c),
+        weight[pl.ds(s * c, c), :],
+        preferred_element_type=jnp.float32,
+    )
+    if s:
+        dot = dsum[...] + dot
+    if s + 1 < parts:
+        dsum[...] = dot
+    else:
+        out_ref[...] = dot.astype(jnp.bfloat16)
+
+
+def project(values, columns, weights, n, collective_id):
     total_rows, depth = values.shape
-    rows, outer = total_rows // n, n // 2
+    rows = total_rows // n
+    levels = n.bit_length() - 1
     c1, c2 = weights[0].shape[1], weights[1].shape[1]
+    gather = len(weights) == 3
     parts = max(p for p in range(1, 8) if c1 % (128 * p) == 0 and c2 % (128 * p) == 0)
-    if gather:
-        out_shape = jax.ShapeDtypeStruct((n, rows, c1), jnp.bfloat16)
-        out_specs = pl.BlockSpec(memory_space=pltpu.VMEM)
-    else:
-        out_shape = [jax.ShapeDtypeStruct((rows, c), jnp.float32) for c in (c1, c2)]
-        out_specs = [pl.BlockSpec(memory_space=pltpu.VMEM)] * 2
     cols = c1 + c2
     wide = cols + EXTRA
     dma = pltpu.SemaphoreType.DMA
+    vmem = pl.BlockSpec(memory_space=pltpu.VMEM)
+    if gather:
+        local = weights[2].shape[1]
+        out_shape = jax.ShapeDtypeStruct((total_rows, local), jnp.bfloat16)
+        out_specs = vmem
+        more = [
+            pltpu.VMEM((c1, local), jnp.bfloat16),
+            pltpu.VMEM((n, rows, c1), jnp.bfloat16),
+            pltpu.VMEM((total_rows, local), jnp.float32),
+            dma((parts,)),
+            dma((parts, n - 1)),
+            dma((parts, n - 1)),
+        ]
+    else:
+        out_shape = [jax.ShapeDtypeStruct((rows, c), jnp.float32) for c in (c1, c2)]
+        out_specs = [vmem] * 2
+        more = []
     return pl.pallas_call(
         functools.partial(project_kernel, n, parts, gather, depth * n),
         out_shape=out_shape,
-        in_specs=[pl.BlockSpec(memory_space=pltpu.VMEM)] * 2
-        + [pl.BlockSpec(memory_space=pl.ANY)] * 2,
+        in_specs=[vmem] * 2 + [pl.BlockSpec(memory_space=pl.ANY)] * len(weights),
         out_specs=out_specs,
         scratch_shapes=[
             pltpu.VMEM((depth, c1), jnp.bfloat16),
             pltpu.VMEM((depth, c2), jnp.bfloat16),
             pltpu.VMEM((n, rows, cols), jnp.bfloat16),
-            pltpu.VMEM((outer, rows, wide), jnp.bfloat16),
-            pltpu.VMEM((outer - 1, rows, wide), jnp.bfloat16),
-            pltpu.VMEM((outer - 1, rows, wide), jnp.bfloat16),
-            pltpu.VMEM((rows, wide), jnp.float32),
+            pltpu.VMEM((n // 2, rows, wide), jnp.bfloat16),
+            pltpu.VMEM((n - 1, rows, wide), jnp.bfloat16),
             pltpu.VMEM((rows, 128), jnp.float32),
             dma((parts, 2)),
-            dma((parts + 1, outer)),
-            dma((parts + 1, outer)),
-            dma((parts + 1, outer - 1)),
-            dma((parts + 1, outer - 1)),
-            dma((parts, outer - 1)),
-            dma((parts, outer - 1)),
-            dma((parts, outer)),
-            dma((parts, outer)),
-        ],
+            dma((parts + 1, n - 1)),
+            dma((parts + 1, n - 1)),
+        ]
+        + more,
         compiler_params=pltpu.CompilerParams(
             collective_id=collective_id, has_side_effects=True, vmem_limit_bytes=VMEM_LIMIT
         ),
@@ -219,56 +292,55 @@
     )(values, columns.reshape(n, rows, EXTRA), *weights)
 
 
-def gather_kernel(n, a_ref, out_ref, own, ns, nr, fs, fr):
-    outer = n // 2
+def gather_kernel(n, parts, a_ref, w_ref, out_ref, w, full, dsum, ls, as_, ar):
+    levels = n.bit_length() - 1
     me = lax.axis_index("gy")
-    o, i = me // 2, lax.rem(me, 2)
-    partner = me + 1 - 2 * i
-    across = [lax.rem(o + k, outer) * 2 + i for k in range(outer)]
-    behind = [lax.rem(o + outer - k, outer) * 2 + i for k in range(outer)]
-    enter("gy", [partner] + across[1:])
-    far_copies, near_copies = [], []
-    for k in range(1, outer):
-        copy = remote(a_ref, out_ref.at[me], fs.at[k - 1], fr.at[k - 1], "gy", across[k])
+    c = a_ref.shape[1] // parts
+    loads = []
+    for s in range(parts):
+        lines = pl.ds(s * c, c)
+        copy = pltpu.make_async_copy(w_ref.at[lines], w.at[lines], ls.at[s])
         copy.start()
-        far_copies.append(copy)
-    copy = remote(a_ref, out_ref.at[me], ns.at[0], nr.at[0], "gy", partner)
-    copy.start()
-    near_copies.append(copy)
-    mine = pltpu.make_async_copy(a_ref, out_ref.at[me], own)
-    mine.start()
-    for k in range(1, outer):
-        far_copies[k - 1].wait_recv()
-        block = out_ref.at[behind[k]]
-        copy = remote(block, block, ns.at[k], nr.at[k], "gy", partner)
-        copy.start()
-        near_copies.append(copy)
-    for copy in near_copies:
-        copy.wait_recv()
-    for copy in far_copies + near_copies:
-        copy.wait_send()
-    mine.wait()
-
-
-def gather_rows(block, n, collective_id):
+        loads.append(copy)
+    full[me] = a_ref[...]
+    enter("gy", [flipped(me, 1 << j) for j in range(levels)])
+    share = Share(me, levels, full, as_, ar)
+    for s in range(parts):
+        share.start(s, bit_order(levels, s, parts), pl.ds(s * c, c))
+    for t in range(parts + levels - 1):
+        for step in range(levels):
+            s = t - step
+            if 0 <= s < parts:
+                share.next(s, step)
+                if step == levels - 1:
+                    loads[s].wait()
+                    add_part(full, w, dsum, out_ref, s, parts)
+    share.end()
+
+
+def gather_project(block, weight, n, collective_id):
     rows, cols = block.shape
-    outer = n // 2
+    local = weight.shape[1]
+    parts = max(p for p in range(1, 5) if cols % (128 * p) == 0)
+    dma = pltpu.SemaphoreType.DMA
+    vmem = pl.BlockSpec(memory_space=pltpu.VMEM)
     return pl.pallas_call(
-        functools.partial(gather_kernel, n),
-        out_shape=jax.ShapeDtypeStruct((n, rows, cols), block.dtype),
-        in_specs=[pl.BlockSpec(memory_space=pltpu.VMEM)],
-        out_specs=pl.BlockSpec(memory_space=pltpu.VMEM),
+        functools.partial(gather_kernel, n, parts),
+        out_shape=jax.ShapeDtypeStruct((n * rows, local), jnp.bfloat16),
+        in_specs=[vmem, pl.BlockSpec(memory_space=pl.ANY)],
+        out_specs=vmem,
         scratch_shapes=[
-            pltpu.SemaphoreType.DMA,
-            pltpu.SemaphoreType.DMA((outer,)),
-            pltpu.SemaphoreType.DMA((outer,)),
-            pltpu.SemaphoreType.DMA((outer - 1,)),
-            pltpu.SemaphoreType.DMA((outer - 1,)),
+            pltpu.VMEM((cols, local), jnp.bfloat16),
+            pltpu.VMEM((n, rows, cols), jnp.bfloat16),
+            pltpu.VMEM((n * rows, local), jnp.float32),
+            dma((parts,)),
+            dma((parts, n - 1)),
+            dma((parts, n - 1)),
         ],
         compiler_params=pltpu.CompilerParams(
             collective_id=collective_id, has_side_effects=True, vmem_limit_bytes=VMEM_LIMIT
         ),
-    )(block)
+    )(block, weight)
 
 
 def residual_kernel(n, p_ref, base_ref, out_ref, near, going, far, *sems):
@@ -432,13 +504,12 @@
     query_cols = query_weight.shape[1]
     heads_local = query_cols // HD
     kv_local = keyval_weight.shape[1] // (2 * HD)
-    hidden = gate_weight.shape[1]
 
     current = (
         tokens.reshape(steps, n, seq_rows, local).transpose(1, 0, 2, 3).reshape(steps * seqs, local)
     )
     values, columns = gained(current, attn_gain)
-    query_part, key_value = project(values, columns, [query_weight, keyval_weight], n, False, 0)
+    query_part, key_value = project(values, columns, [query_weight, keyval_weight], n, 0)
     positions = (cache_lengths[None, :] + jnp.arange(steps)[:, None]).astype(jnp.float32)
     queries = rotary(
         query_part.reshape(steps, seq_rows, heads_local, HD), positions
@@ -455,15 +526,12 @@
         new_values.transpose(1, 0, 2, 3),
     )
     attended = attended.transpose(2, 0, 1, 3, 4).reshape(steps * seq_rows, query_cols)
-    gathered = gather_rows(attended, n, 1).reshape(steps * seqs, query_cols)
-    partial_out = jnp.dot(gathered, out_weight, preferred_element_type=jnp.float32)
-    resid = add_residual(partial_out.astype(jnp.bfloat16), current, m, 2)
+    partial_out = gather_project(attended, out_weight, n, 1)
+    resid = add_residual(partial_out, current, m, 2)
 
     values, columns = gained(resid, ffn_gain)
-    activated = project(values, columns, [gate_weight, up_weight], n, True, 3)
-    gathered = activated.reshape(steps * seqs, hidden)
-    partial_down = jnp.dot(gathered, down_weight, preferred_element_type=jnp.float32)
-    result = add_residual(partial_down.astype(jnp.bfloat16), resid, m, 5)
+    partial_down = project(values, columns, [gate_weight, up_weight, down_weight], n, 3)
+    result = add_residual(partial_down, resid, m, 5)
     return (
         result.reshape(n, steps, seq_rows, local).transpose(1, 0, 2, 3).reshape(steps, seqs, local)
     )

time: 323 us -> 294 us (0.910)
  Pallas kernels: 262 us -> 246 us
  matrix products: 35.5 us -> 22.4 us
    pallas_call x2, Pallas kernels: 186 us -> 169 us  [project(): pl.pallas_call(functools.partial(project_kernel, n, parts, gather, depth...]
    dot_general x2 -> x0, matrix products: 13.1 us -> none  [the longest x1 6.96 us: per_device(): jnp.dot(gathered, down_weight, preferred_element_type=jnp.float32)]
where the time goes in v3:
time: 294 us; the launch traced here: 293 us
  Pallas kernels  246 us (84%)
  matrix products  22.4 us (8%)
  other arithmetic  18.1 us (6%)
  local copies, waits for them, and re-layouts  6.67 us (2%)
    pallas_call x2, Pallas kernels, project(): pl.pallas_call(functools.partial(project_kernel, n, parts, gather, depth...  169 us
    pallas_call x2, Pallas kernels, add_residual(): pl.pallas_call(functools.partial(residual_kernel, n), out_shape=jax.Shape...  42 us
    pallas_call x1, Pallas kernels, gather_project(): pl.pallas_call(functools.partial(gather_kernel, n, parts), out_shape=jax....  34.8 us
    dot_general x1, matrix products, attend(): jnp.einsum('sgjd,stgd->sgjt', flat, cached_keys, preferred_element_type=j...  12.3 us
    dot_general x1, matrix products, attend(): jnp.einsum('sgjt,stgd->sgjd', cached_probs, cached_values, preferred_elem...  9.38 us

profile of v3, /device:TPU:0, one launch (start us, length us, event | category | flops | bytes accessed | tf_op | source)
XLA Modules:
  0.0 293.5 jit_solution(10748612556372204922)
XLA Ops:
  0.1 0.7 add_convert_fusion.2
  0.8 0.7 convert_element_type.140
  1.5 0.7 convert_element_type.154
  2.1 1.5 multiply_reduce_fusion.1
  3.7 0.7 iota_compare_fusion
  4.5 0.2 multiply_cosine_fusion
  4.8 0.2 copy.42
  4.9 0.2 copy.40
  5.3 0.8 maximum_maximum_fusion.sq_ref
  6.0 2.5 fusion.32
  8.5 1.2 fusion.7.x_ref
  9.8 44.8 %shard_map.118 = (f32[64,2048]{1,0:T(8,128)}, f32[64,512]{1,0:T(8,128)}) custom-call(bf16[512,1024]{1,0:T(8,128)(2,1)} %fusion.7.x_ref, bf16[8,64,128]{2,1,0:T(8,128)(2,1)} %maximum_maximum_fusion.sq_ref, bf16[1024,2048]{1,0:T(8,128)(2,1)} %w1_ref.2, bf16[1024,512]{1,0:T(8,128)(2,1)} %w2_ref.2), custom_call_target="tpu_custom_call" | custom-call | flops 2684354560 | bytes 5242880 | tf_op jit(solution)/shard_map/pallas_call | solution.py:269
  54.6 1.1 copy.59
  55.7 0.2 fusion.16
  56.0 1.0 reshape.216
  57.2 0.2 subtract_convert_fusion.3
  57.4 0.4 fusion.33
  57.8 12.3 %fusion.4 = (f32[32,2,16]{2,1,0:T(2,128)S(1)}, f32[32,2,16,1024]{3,2,1,0:T(8,128)}) fusion(pred[32,1024]{1,0:T(8,128)(4,1)S(1)} %iota_compare_fusion, bf16[32,1024,2,128]{3,2,1,0:T(2,128)(2,1)} %param.14, bf16[2,32,2,8,64]{4,3,2,1,0:T(8,128)(2,1)S(1)} %get-tuple-element.12, bf16[2,32,2,8,64]{4,3,2,1,0:T(8,128)(2,1)S(1)} %get-tuple-element.11), kind=kOutput, calls=%fused_computation.7 | convolution fusion | flops 272104448 | bytes 21270528 | tf_op jit(solution)/shard_map/sgjd,stgd->sgjt/dot_general | solution.py:445
  70.3 3.7 %fusion.5 = f32[32,2,16]{2,1,0:T(2,128)S(1)} fusion(f32[32,2,16,1024]{3,2,1,0:T(8,128)} %get-tuple-element.18, f32[32,2,16]{2,1,0:T(2,128)S(1)} %max.8, pred[32,1024]{1,0:T(8,128)(4,1)S(1)} %iota_compare_fusion), kind=kLoop, calls=%fused_computation.8 | loop fusion | flops 4193280 | bytes 4235264 | tf_op jit(solution)/shard_map/reduce_sum | solution.py:462
  74.0 9.4 %fusion = f32[32,2,16,128]{3,2,1,0:T(8,128)S(1)} fusion(bf16[32,1024,2,128]{3,2,1,0:T(2,128)(2,1)} %param.15, f32[32,2,16,1024]{3,2,1,0:T(8,128)S(1)} %copy-done, f32[32,2,16]{2,1,0:T(2,128)S(1)} %add.44, f32[32,2,16]{2,1,0:T(2,128)S(1)} %max.8, pred[32,1024]{1,0:T(8,128)(4,1)S(1)} %iota_compare_fusion), kind=kOutput, calls=%fused_computation | convolution fusion | flops 273678336 | bytes 21536768 | tf_op jit(solution)/shard_map/sgjt,stgd->sgjd/dot_general | solution.py:467
  83.4 0.3 fusion.14
  83.7 0.8 reshape.217.a_ref
  84.5 34.8 %shard_map.119 = bf16[512,1024]{1,0:T(8,128)(2,1)} custom-call(bf16[64,2048]{1,0:T(8,128)(2,1)} %reshape.217.a_ref, bf16[2048,1024]{1,0:T(8,128)(2,1)} %w_ref.1), custom_call_target="tpu_custom_call" | custom-call | tf_op jit(solution)/shard_map/pallas_call | solution.py:327
  119.3 21.0 %shard_map.120.base_ref = bf16[4,128,1024]{2,1,0:T(8,128)(2,1)} custom-call(bf16[4,128,1024]{2,1,0:T(8,128)(2,1)} %bitcast.64, bf16[4,128,1024]{2,1,0:T(8,128)(2,1)} %bitcast.63), custom_call_target="tpu_custom_call" | custom-call | tf_op jit(solution)/shard_map/pallas_call | solution.py:403
  140.3 1.5 multiply_reduce_fusion
  141.9 0.2 copy.54
  142.1 0.2 copy.52
  142.4 0.8 maximum_maximum_fusion.1.sq_ref
  143.2 2.4 fusion.6.x_ref
  145.6 124.5 %shard_map.121 = bf16[512,1024]{1,0:T(8,128)(2,1)} custom-call(bf16[512,1024]{1,0:T(8,128)(2,1)} %fusion.6.x_ref, bf16[8,64,128]{2,1,0:T(8,128)(2,1)} %maximum_maximum_fusion.1.sq_ref, bf16[1024,3584]{1,0:T(8,128)(2,1)} %w1_ref.3, bf16[1024,3584]{1,0:T(8,128)(2,1)} %w2_ref.3, bf16[3584,1024]{1,0:T(8,128)(2,1)} %refs_0_.1), custom_call_target="tpu_custom_call" | custom-call | flops 7516192768 | bytes 14680064 | tf_op jit(solution)/shard_map/pallas_call | solution.py:269
  270.2 21.0 %shard_map.122 = bf16[4,128,1024]{2,1,0:T(8,128)(2,1)} custom-call(bf16[4,128,1024]{2,1,0:T(8,128)(2,1)} %bitcast.66, bf16[4,128,1024]{2,1,0:T(8,128)(2,1)} %shard_map.120.base_ref), custom_call_target="tpu_custom_call" | custom-call | tf_op jit(solution)/shard_map/pallas_call | solution.py:403
  291.2 2.3 copy.55
  (24 shorter events, 1.1 us)
Async XLA Ops:
  70.1 3.9 %copy-start = (f32[32,2,16,1024]{3,2,1,0:T(8,128)S(1)}, f32[32,2,16,1024]{3,2,1,0:T(8,128)}, u32[]{:S(2)}) copy-start(f32[32,2,16,1024]{3,2,1,0:T(8,128)} %get-tuple-element.18) | copy-start | bytes 12582916

commit v4 on v3

--- a/solution.py
+++ b/solution.py
@@ -11,6 +11,7 @@
 HD = 128
 GROUP = 8
 EXTRA = 128
+HALVES = 2
 VMEM_LIMIT = 56 * 1024 * 1024
 MESH = pl.DeviceIdType.MESH
 
@@ -90,16 +91,16 @@
             copy.wait_send()
 
 
-def project_kernel(n, parts, gather, width, x_ref, sq_ref, w1_ref, w2_ref, *refs):
+def project_kernel(n, parts, gather, width, v_ref, gain_ref, w1_ref, w2_ref, *refs):
     if gather:
         w3_ref, out_ref, w3, full, dsum, ls, as_, ar = refs[0], refs[1], *refs[-6:]
         refs = refs[2:-6]
     else:
         out1_ref, out2_ref, refs = refs[0], refs[1], refs[2:]
-    w1, w2, p_ref, cur, got, scale, ws, ss, rs = refs
+    w1, w2, x_ref, sq_ref, p_ref, cur, got, scale, ws, ss, rs = refs
     levels = n.bit_length() - 1
     me = lax.axis_index("gy")
-    rows = sq_ref.shape[1]
+    rows = v_ref.shape[0] // n
     a, b = w1.shape[1] // parts, w2.shape[1] // parts
     size = a + b
     loads, late_loads = [], []
@@ -119,6 +120,13 @@
             copy.start()
             late_loads.append(copy)
         share = Share(me, levels, full, as_, ar)
+    values = v_ref[...].astype(jnp.float32)
+    x_ref[...] = (values * gain_ref[...]).astype(jnp.bfloat16)
+    squares = jnp.sum(values * values, axis=1, keepdims=True)
+    high = squares.astype(jnp.bfloat16).astype(jnp.float32)
+    lane = lax.broadcasted_iota(jnp.int32, (n * rows, EXTRA), 1)
+    columns = jnp.where(lane == 0, high, jnp.where(lane == 1, squares - high, 0.0))
+    sq_ref[...] = columns.astype(jnp.bfloat16).reshape(n, rows, EXTRA)
     segments = [(sq_ref, 0, parts * size, EXTRA)]
     segments += [(p_ref, s * size, s * size, size) for s in range(parts)]
     orders = [list(range(levels))] + [bit_order(levels, s, parts) for s in range(parts)]
@@ -239,7 +247,7 @@
         out_ref[...] = dot.astype(jnp.bfloat16)
 
 
-def project(values, columns, weights, n, collective_id):
+def project(values, gain, weights, n, collective_id):
     total_rows, depth = values.shape
     rows = total_rows // n
     levels = n.bit_length() - 1
@@ -274,6 +282,8 @@
         scratch_shapes=[
             pltpu.VMEM((depth, c1), jnp.bfloat16),
             pltpu.VMEM((depth, c2), jnp.bfloat16),
+            pltpu.VMEM((total_rows, depth), jnp.bfloat16),
+            pltpu.VMEM((n, rows, EXTRA), jnp.bfloat16),
             pltpu.VMEM((n, rows, cols), jnp.bfloat16),
             pltpu.VMEM((n // 2, rows, wide), jnp.bfloat16),
             pltpu.VMEM((n - 1, rows, wide), jnp.bfloat16),
@@ -289,7 +299,7 @@
         cost_estimate=pl.CostEstimate(
             flops=2 * total_rows * depth * cols, bytes_accessed=2 * depth * cols, transcendentals=0
         ),
-    )(values, columns.reshape(n, rows, EXTRA), *weights)
+    )(values, gain.astype(jnp.float32).reshape(1, depth), *weights)
 
 
 def gather_kernel(n, parts, a_ref, w_ref, out_ref, w, full, dsum, ls, as_, ar):
@@ -354,6 +364,9 @@
     enter("gx", [partner] + [across[k] * 2 + i for k in range(1, outer)])
     order = [(k + 1) % outer for k in range(outer)]
     copies, near_copies, far_copies, share_far, share_near = [], {}, {}, {}, {}
+    width = p_ref.shape[2] // HALVES
+    spans = [pl.ds(h * width, width) for h in range(HALVES)]
+    own = {}
 
     def send(src, dst, send_sem, recv_sem, device):
         copy = remote(src, dst, send_sem, recv_sem, "gx", device)
@@ -361,34 +374,49 @@
         copies.append(copy)
         return copy
 
-    for k in order:
-        near_copies[k] = send(
-            p_ref.at[across[k] * 2 + 1 - i], near.at[k], ns.at[k], nr.at[k], partner
-        )
-    for k in order:
-        near_copies[k].wait_recv()
-        total = p_ref[across[k] * 2 + i].astype(jnp.float32) + near[k].astype(jnp.float32)
-        if k:
-            going[k - 1] = total.astype(jnp.bfloat16)
-            far_copies[k] = send(
-                going.at[k - 1],
-                far.at[k - 1],
-                fs.at[k - 1],
-                fr.at[k - 1],
-                across[k] * 2 + i,
+    for h, cols in enumerate(spans):
+        for k in order:
+            near_copies[h, k] = send(
+                p_ref.at[across[k] * 2 + 1 - i, :, cols],
+                near.at[k, :, cols],
+                ns.at[h, k],
+                nr.at[h, k],
+                partner,
             )
-    for k in range(1, outer):
-        far_copies[k].wait_recv()
-        total = total + far[k - 1].astype(jnp.float32)
-    out_ref[me] = (base_ref[me].astype(jnp.float32) + total).astype(jnp.bfloat16)
-    block = out_ref.at[me]
-    for k in range(1, outer):
-        share_far[k] = send(block, block, as_.at[k - 1], ar.at[k - 1], across[k] * 2 + i)
-    share_near[0] = send(block, block, bs.at[0], br.at[0], partner)
-    for k in range(1, outer):
-        share_far[k].wait_recv()
-        block = out_ref.at[behind[k]]
-        share_near[k] = send(block, block, bs.at[k], br.at[k], partner)
+    for h, cols in enumerate(spans):
+        for k in order:
+            near_copies[h, k].wait_recv()
+            total = p_ref[across[k] * 2 + i, :, cols].astype(jnp.float32) + near[
+                k, :, cols
+            ].astype(jnp.float32)
+            if k:
+                going[k - 1, :, cols] = total.astype(jnp.bfloat16)
+                far_copies[h, k] = send(
+                    going.at[k - 1, :, cols],
+                    far.at[k - 1, :, cols],
+                    fs.at[h, k - 1],
+                    fr.at[h, k - 1],
+                    across[k] * 2 + i,
+                )
+            else:
+                own[h] = total + base_ref[me, :, cols].astype(jnp.float32)
+    for h, cols in enumerate(spans):
+        total = own[h]
+        for k in range(1, outer):
+            far_copies[h, k].wait_recv()
+            total = total + far[k - 1, :, cols].astype(jnp.float32)
+        out_ref[me, :, cols] = total.astype(jnp.bfloat16)
+        block = out_ref.at[me, :, cols]
+        for k in range(1, outer):
+            share_far[h, k] = send(
+                block, block, as_.at[h, k - 1], ar.at[h, k - 1], across[k] * 2 + i
+            )
+        share_near[h, 0] = send(block, block, bs.at[h, 0], br.at[h, 0], partner)
+    for h, cols in enumerate(spans):
+        for k in range(1, outer):
+            share_far[h, k].wait_recv()
+            block = out_ref.at[behind[k], :, cols]
+            share_near[h, k] = send(block, block, bs.at[h, k], br.at[h, k], partner)
     for copy in share_near.values():
         copy.wait_recv()
     for copy in copies:
@@ -410,9 +438,9 @@
             pltpu.VMEM((outer - 1,) + shape[1:], jnp.bfloat16),
             pltpu.VMEM((outer - 1,) + shape[1:], jnp.bfloat16),
         ]
-        + [dma((outer,))] * 2
-        + [dma((outer - 1,))] * 4
-        + [dma((outer,))] * 2,
+        + [dma((HALVES, outer))] * 2
+        + [dma((HALVES, outer - 1))] * 4
+        + [dma((HALVES, outer))] * 2,
         compiler_params=pltpu.CompilerParams(
             collective_id=collective_id, has_side_effects=True, vmem_limit_bytes=VMEM_LIMIT
         ),
@@ -471,17 +499,6 @@
         "sgje,segd->sgjd", recent_probs, extra_values, preferred_element_type=jnp.float32
     )
     return mixed.reshape(seqs, kv, steps, GROUP, HD).astype(jnp.bfloat16)
-
-
-def gained(values, gain):
-    wide = values.astype(jnp.float32)
-    squares = jnp.sum(wide * wide, axis=1, keepdims=True)
-    high = squares.astype(jnp.bfloat16)
-    low = (squares - high.astype(jnp.float32)).astype(jnp.bfloat16)
-    pad = jnp.zeros((values.shape[0], EXTRA - 2), jnp.bfloat16)
-    return (wide * gain.astype(jnp.float32)).astype(jnp.bfloat16), jnp.concatenate(
-        [high, low, pad], axis=1
-    )
 
 
 def per_device(
@@ -508,8 +525,7 @@
     current = (
         tokens.reshape(steps, n, seq_rows, local).transpose(1, 0, 2, 3).reshape(steps * seqs, local)
     )
-    values, columns = gained(current, attn_gain)
-    query_part, key_value = project(values, columns, [query_weight, keyval_weight], n, 0)
+    query_part, key_value = project(current, attn_gain, [query_weight, keyval_weight], n, 0)
     positions = (cache_lengths[None, :] + jnp.arange(steps)[:, None]).astype(jnp.float32)
     queries = rotary(
         query_part.reshape(steps, seq_rows, heads_local, HD), positions
@@ -529,8 +545,7 @@
     partial_out = gather_project(attended, out_weight, n, 1)
     resid = add_residual(partial_out, current, m, 2)
 
-    values, columns = gained(resid, ffn_gain)
-    partial_down = project(values, columns, [gate_weight, up_weight, down_weight], n, 3)
+    partial_down = project(resid, ffn_gain, [gate_weight, up_weight, down_weight], n, 3)
     result = add_residual(partial_down, resid, m, 5)
     return (
         result.reshape(n, steps, seq_rows, local).transpose(1, 0, 2, 3).reshape(steps, seqs, local)

time: 294 us -> 282 us (0.959)
  other arithmetic: 18.1 us -> 8.26 us
  Pallas kernels: 246 us -> 243 us
    convert_element_type x8 -> x0, other arithmetic: 5.13 us -> none  [the longest x2 3.69 us: gained(): (wide * gain.astype(jnp.float32)).astype(jnp.bfloat16)]
    pallas_call x2, Pallas kernels: 42 us -> 37.8 us  [add_residual(): pl.pallas_call(functools.partial(residual_kernel, n), out_shape=jax.Shape...]
    reduce_sum x2 -> x0, other arithmetic: 3.01 us -> none  [gained(): squares = jnp.sum(wide * wide, axis=1, keepdims=True)]
where the time goes in v4:
time: 282 us; the launch traced here: 281 us
  Pallas kernels  243 us (86%)
  matrix products  22.5 us (8%)
  other arithmetic  8.26 us (3%)
  local copies, waits for them, and re-layouts  7.79 us (3%)
    pallas_call x2, Pallas kernels, project(): pl.pallas_call(functools.partial(project_kernel, n, parts, gather, depth...  170 us
    pallas_call x2, Pallas kernels, add_residual(): pl.pallas_call(functools.partial(residual_kernel, n), out_shape=jax.Shape...  37.8 us
    pallas_call x1, Pallas kernels, gather_project(): pl.pallas_call(functools.partial(gather_kernel, n, parts), out_shape=jax....  35.1 us
    dot_general x1, matrix products, attend(): jnp.einsum('sgjd,stgd->sgjt', flat, cached_keys, preferred_element_type=j...  12.3 us
    dot_general x1, matrix products, attend(): jnp.einsum('sgjt,stgd->sgjd', cached_probs, cached_values, preferred_elem...  9.52 us

profile of v4, /device:TPU:0, one launch (start us, length us, event | category | flops | bytes accessed | tf_op | source)
XLA Modules:
  0.0 281.3 jit_solution(16135049890538289800)
XLA Ops:
  0.0 0.7 add_convert_fusion.2
  0.7 1.3 reshape.151
  1.9 1.3 reshape.153
  3.2 0.7 iota_compare_fusion
  4.0 0.2 multiply_cosine_fusion
  4.2 2.3 copy.24
  6.5 44.8 %shard_map.118 = (f32[64,2048]{1,0:T(8,128)}, f32[64,512]{1,0:T(8,128)}) custom-call(bf16[512,1024]{1,0:T(8,128)(2,1)} %bitcast.55, f32[1,1024]{1,0:T(1,128)} %bitcast.65, bf16[1024,2048]{1,0:T(8,128)(2,1)} %w1_ref.2, bf16[1024,512]{1,0:T(8,128)(2,1)} %w2_ref.2), custom_call_target="tpu_custom_call" | custom-call | flops 2684354560 | bytes 5242880 | tf_op jit(solution)/shard_map/pallas_call | solution.py:277
  51.3 1.1 copy.38
  52.4 0.2 fusion.14
  52.7 1.0 reshape.143
  53.7 0.1 slice.30
  53.8 0.1 copy.64
  53.9 0.2 subtract_convert_fusion.1
  54.1 0.4 fusion.30
  54.5 12.3 %fusion.4 = (f32[32,2,16]{2,1,0:T(2,128)S(1)}, f32[32,2,16,1024]{3,2,1,0:T(8,128)}) fusion(pred[32,1024]{1,0:T(8,128)(4,1)S(1)} %iota_compare_fusion, bf16[32,1024,2,128]{3,2,1,0:T(2,128)(2,1)} %param.14, bf16[2,32,2,8,64]{4,3,2,1,0:T(8,128)(2,1)S(1)} %get-tuple-element.10, bf16[2,32,2,8,64]{4,3,2,1,0:T(8,128)(2,1)S(1)} %get-tuple-element.9), kind=kOutput, calls=%fused_computation.7 | convolution fusion | flops 272104448 | bytes 21270528 | tf_op jit(solution)/shard_map/sgjd,stgd->sgjt/dot_general | solution.py:473
  66.7 0.0 copy-start
  66.8 0.1 fusion.20
  66.9 3.5 %fusion.5 = f32[32,2,16]{2,1,0:T(2,128)S(1)} fusion(f32[32,2,16,1024]{3,2,1,0:T(8,128)} %get-tuple-element.16, f32[32,2,16]{2,1,0:T(2,128)S(1)} %max.8, pred[32,1024]{1,0:T(8,128)(4,1)S(1)} %iota_compare_fusion), kind=kLoop, calls=%fused_computation.8 | loop fusion | flops 4193280 | bytes 4235264 | tf_op jit(solution)/shard_map/reduce_sum | solution.py:490
  70.4 0.0 copy-done
  70.5 9.5 %fusion = f32[32,2,16,128]{3,2,1,0:T(8,128)S(1)} fusion(bf16[32,1024,2,128]{3,2,1,0:T(2,128)(2,1)} %param.15, f32[32,2,16,1024]{3,2,1,0:T(8,128)S(1)} %copy-done, f32[32,2,16]{2,1,0:T(2,128)S(1)} %add.44, f32[32,2,16]{2,1,0:T(2,128)S(1)} %max.8, pred[32,1024]{1,0:T(8,128)(4,1)S(1)} %iota_compare_fusion), kind=kOutput, calls=%fused_computation | convolution fusion | flops 273678336 | bytes 21536768 | tf_op jit(solution)/shard_map/sgjt,stgd->sgjd/dot_general | solution.py:495
  80.0 0.3 fusion.12
  80.3 0.8 reshape.144.a_ref
  81.2 35.1 %shard_map.119 = bf16[512,1024]{1,0:T(8,128)(2,1)} custom-call(bf16[64,2048]{1,0:T(8,128)(2,1)} %reshape.144.a_ref, bf16[2048,1024]{1,0:T(8,128)(2,1)} %w_ref.1), custom_call_target="tpu_custom_call" | custom-call | tf_op jit(solution)/shard_map/pallas_call | solution.py:337
  116.3 19.2 %shard_map.120.base_ref = bf16[4,128,1024]{2,1,0:T(8,128)(2,1)} custom-call(bf16[4,128,1024]{2,1,0:T(8,128)(2,1)} %bitcast.58, bf16[4,128,1024]{2,1,0:T(8,128)(2,1)} %bitcast.56), custom_call_target="tpu_custom_call" | custom-call | tf_op jit(solution)/shard_map/pallas_call | solution.py:431
  135.5 124.9 %shard_map.121 = bf16[512,1024]{1,0:T(8,128)(2,1)} custom-call(bf16[512,1024]{1,0:T(8,128)(2,1)} %bitcast.54, f32[1,1024]{1,0:T(1,128)} %bitcast.64, bf16[1024,3584]{1,0:T(8,128)(2,1)} %w1_ref.3, bf16[1024,3584]{1,0:T(8,128)(2,1)} %w2_ref.3, bf16[3584,1024]{1,0:T(8,128)(2,1)} %refs_0_.1), custom_call_target="tpu_custom_call" | custom-call | flops 7516192768 | bytes 14680064 | tf_op jit(solution)/shard_map/pallas_call | solution.py:277
  260.4 18.6 %shard_map.122 = bf16[4,128,1024]{2,1,0:T(8,128)(2,1)} custom-call(bf16[4,128,1024]{2,1,0:T(8,128)(2,1)} %bitcast.59, bf16[4,128,1024]{2,1,0:T(8,128)(2,1)} %shard_map.120.base_ref), custom_call_target="tpu_custom_call" | custom-call | tf_op jit(solution)/shard_map/pallas_call | solution.py:431
  279.0 2.3 copy.34
  (9 shorter events, 0.2 us)
Async XLA Ops:
  66.7 3.7 %copy-start = (f32[32,2,16,1024]{3,2,1,0:T(8,128)S(1)}, f32[32,2,16,1024]{3,2,1,0:T(8,128)}, u32[]{:S(2)}) copy-start(f32[32,2,16,1024]{3,2,1,0:T(8,128)} %get-tuple-element.16) | copy-start | bytes 12582916
